TPU v7x, 512 devices: a whole 4x4x16 slice. The times are simulated.
512 devices in a mesh: req: 16 (over y, x), head: 4 (over z_lo), exp: 8 (over z_hi, core).
Axes of the slice: x: 4, y: 4, z: 16 (z_hi: 4, z_lo: 4; z = z_hi * 4 + z_lo), core: 2. Of those that a mesh axis runs over, the one named last changes fastest.
Arguments:
- moe_input: bfloat16 [768, 7168], P(('req', 'head'), 'exp'), may hold values from -6 to 6
- route_ids: int32 [768, 3], P(('req', 'head')), may hold values from 0 to 23, all different within a row; in each aligned block of 12 rows (0 to 11, 12 to 23, ...) at most 2 rows name the same one
- route_weight: float32 [768, 3], P(('req', 'head')), may hold values from 0.1 to 1
- w_up: bfloat16 [24, 2560, 7168], P('exp', ('req', 'head')), may hold values from -0.0625 to 0.0625
- w_down: bfloat16 [24, 2560, 7168], P('exp', None, ('req', 'head')), may hold values from -0.125 to 0.125
- queries: bfloat16 [512, 64, 256], P(('req', 'head', 'exp')), may hold values from -24 to 24
- keys: bfloat16 [512, 1024, 256], P(('req', 'head', 'exp')), may hold values from -6 to 6
- values: bfloat16 [512, 1024, 256], P(('req', 'head', 'exp')), may hold values from -6 to 6
Outputs:
- moe_output: bfloat16 [768, 7168], P(('req', 'head'), 'exp')
- context: bfloat16 [512, 64, 256], P(('req', 'head', 'exp'))
Inputs may be any that keep to these rules, and one draw needn't show every extreme that they name: `route_ids`: the 3 ids of a row differ. In each aligned block of 12 rows (the rows of one device) no expert is named by more than 2 rows, a bound that some block reaches.
All inputs are finite; a program needn't handle non-finite values.
Results may differ from a plain program's by a relative error of at most 0.0047.
Values may be sent and summed in bfloat16 or wider, within the bound.
A program may use at most 64 MiB of HBM per device.

v0:
```python
import math

import jax
import jax.numpy as jnp
from jax import lax
from jax.sharding import PartitionSpec as P


def attend(queries, keys, values):
    score_scale = 1.0 / math.sqrt(queries.shape[2])
    scores = (
        jnp.einsum("rhd,rld->rhl", queries, keys, preferred_element_type=jnp.float32) * score_scale
    )
    row_max = jnp.max(scores, axis=2, keepdims=True)
    weights = jnp.exp(scores - row_max)
    row_total = jnp.sum(weights, axis=2)
    weighted = jnp.einsum(
        "rhl,rld->rhd", weights.astype(jnp.bfloat16), values, preferred_element_type=jnp.float32
    )
    return (weighted / row_total[:, :, None]).astype(jnp.bfloat16)


def shards(moe_input, route_ids, route_weight, w_up, w_down, queries, keys, values):
    tok_rows, width_part = moe_input.shape
    top_count = route_ids.shape[1]
    exp_count = lax.axis_size("exp")
    source_count = lax.axis_size(("req", "head"))
    local_experts = w_up.shape[0]
    experts_all = local_experts * exp_count
    capacity = max(2, (tok_rows * top_count + experts_all - 1) // experts_all)
    onehot = (
        route_ids[:, :, None] == jnp.arange(experts_all, dtype=jnp.int32)[None, None, :]
    ).astype(jnp.float32)
    per_row = onehot.sum(axis=1)
    row_index = jnp.arange(tok_rows, dtype=jnp.int32)
    below_mask = (row_index[:, None] > row_index[None, :]).astype(jnp.float32)
    before = jnp.dot(below_mask, per_row, precision=lax.Precision.HIGHEST)
    slot_rank = jnp.sum(onehot * before[:, None, :], axis=2)
    slot_index = jnp.arange(capacity, dtype=jnp.float32)
    choose_mask = onehot[:, :, :, None] * (
        slot_rank[:, :, None, None] == slot_index[None, None, None, :]
    ).astype(jnp.float32)
    placing = choose_mask.sum(axis=1)
    combine = jnp.einsum("tk,tkec->tec", route_weight, choose_mask).reshape(
        tok_rows, experts_all * capacity
    )
    outgoing = jnp.einsum(
        "tec,td->ecd", placing.astype(jnp.bfloat16), moe_input, preferred_element_type=jnp.float32
    )
    outgoing = outgoing.astype(jnp.bfloat16).reshape(exp_count, local_experts, capacity, width_part)
    everyone = lax.all_gather(outgoing, ("req", "head"), axis=2, tiled=True)
    arrived = lax.all_to_all(everyone, "exp", split_axis=0, concat_axis=3, tiled=True)
    raised = jnp.einsum("ekd,efd->ekf", arrived[0], w_up, preferred_element_type=jnp.float32)
    hidden = jax.nn.silu(raised).astype(jnp.bfloat16)
    result = jnp.einsum(
        "esf,efd->esd",
        lax.all_gather(hidden, ("req", "head"), axis=2, tiled=True),
        w_down,
        preferred_element_type=jnp.float32,
    ).astype(jnp.bfloat16)
    result = result.reshape(local_experts, source_count, capacity, w_down.shape[2])
    returned = lax.all_to_all(
        lax.all_to_all(result, ("req", "head"), split_axis=1, concat_axis=3, tiled=True),
        "exp",
        split_axis=3,
        concat_axis=0,
        tiled=True,
    )
    returned = returned.reshape(experts_all * capacity, width_part).astype(jnp.float32)
    expert_sum = jnp.dot(combine, returned, precision=lax.Precision.HIGHEST)
    moe_output = (moe_input.astype(jnp.float32) + expert_sum).astype(jnp.bfloat16)
    context = attend(queries, keys, values)
    return (moe_output, context)


def solution(mesh):
    placed = (
        P(("req", "head"), "exp"),
        P(("req", "head"), None),
        P(("req", "head"), None),
        P("exp", ("req", "head"), None),
        P("exp", None, ("req", "head")),
        P(("req", "head", "exp"), None, None),
        P(("req", "head", "exp"), None, None),
        P(("req", "head", "exp"), None, None),
    )
    return jax.shard_map(
        shards,
        mesh=mesh,
        in_specs=placed,
        out_specs=(P(("req", "head"), "exp"), P(("req", "head", "exp"), None, None)),
        check_vma=False,
    )
```

profile of v0, /device:TPU:1, one launch (start us, length us, event | category | flops | bytes accessed | tf_op | source)
XLA Modules:
  0.0 1097.4 jit_solution(10342381640757228963)
XLA Ops:
  7.2 0.0 copy-start
  7.2 0.0 all-gather.3.cloned.1.call-start
  7.2 0.9 fusion.14
  8.1 0.8 fusion.12
  8.9 0.8 copy.66
  9.6 0.1 fusion.16
  9.8 0.8 select_reduce_fusion
  10.6 0.1 copy.48
  10.7 0.1 fusion.13
  10.8 0.2 multiply_reduce_fusion
  11.0 0.9 convolution_convert_fusion.1
  11.9 0.1 copy.50
  12.0 0.6 copy.51
  12.6 0.0 all-gather.3.cloned.1.call-update
  12.7 0.0 all-gather.5.cloned.1.call-start
  12.7 335.7 %all-gather.3.cloned.1.call-done = bf16[8,3,128,896]{3,0,1,2:T(8,128)(2,1)} async-done(((bf16[8,3,2,896]{3,0,1,2:T(8,128)(2,1)}), bf16[8,3,128,896]{3,0,1,2:T(8,128)(2,1)}) %all-gather.3.cloned.1.call-update) | async-done | bytes 5505040 | tf_op jit(solution)/shard_map/all_gather | solution.py:51
  348.4 3.5 copy.52
  352.0 290.7 %all_to_all.48 = bf16[8,3,128,896]{3,2,1,0:T(8,128)(2,1)S(1)} all-to-all(bf16[8,3,128,896]{3,2,1,0:T(8,128)(2,1)S(1)} %copy.52), channel_id=1, replica_groups=mesh['req'=16,'head'=4,'exp'=8] {'exp'}, dimensions={0} | all-to-all | bytes 11010048 | tf_op jit(solution)/shard_map/all_to_all | solution.py:52
  642.7 5.6 copy.53
  648.2 0.0 copy-start.1
  648.2 9.2 squeeze.3
  657.4 0.0 copy-done.1
  657.4 5.2 multiply_convert_fusion
  662.6 0.0 all-gather.5.cloned.1.call-update
  662.6 305.8 %all-gather.5.cloned.1.call-done = bf16[3,128,2560]{1,2,0:T(8,128)(2,1)} async-done(((bf16[3,128,40]{1,2,0:T(8,128)(2,1)}), bf16[3,128,2560]{1,2,0:T(8,128)(2,1)}) %all-gather.5.cloned.1.call-update) | async-done | bytes 1966096 | tf_op jit(solution)/shard_map/all_gather | solution.py:57
  968.4 0.0 copy-done
  968.4 2.2 convolution_convert_fusion
  970.6 0.1 copy.54
  970.7 0.1 copy.55
  970.8 16.8 %all_to_all.49 = bf16[3,64,2,112]{3,2,0,1:T(2,128)(2,1)S(1)} all-to-all(bf16[3,64,2,112]{3,2,0,1:T(2,128)(2,1)S(1)} %copy.55), channel_id=1, replica_groups=mesh['req'=16,'head'=4,'exp'=8] {'req','head'}, dimensions={1} | all-to-all | bytes 172032 | tf_op jit(solution)/shard_map/all_to_all | solution.py:63
  987.6 5.9 copy.64
  993.5 0.0 copy-start.3
  993.5 0.0 copy-start.5
  993.5 0.0 copy-start.2
  993.5 8.9 reshape.73
  1002.4 57.3 %all-to-all-start.2 = ((bf16[8,2,2688]{2,1,0:T(2,128)(2,1)}), bf16[8,2,2688]{2,1,0:T(2,128)(2,1)S(1)}, u32[]{:S(2)}, u32[]{:S(2)}) async-start(bf16[8,2,2688]{2,1,0:T(2,128)(2,1)} %reshape.73), calls=%async_computation.2 | async-start | bytes 172032 | tf_op jit(solution)/shard_map/all_to_all | solution.py:62
  1059.7 0.0 copy-done.3
  1059.7 0.0 copy-done.5
  1059.7 0.4 fusion.17
  1060.1 0.1 copy.63
  1060.2 0.2 fusion.5
  1060.4 0.0 copy-done.2
  1060.4 0.9 fusion.2
  1061.3 10.7 all-to-all-done.2
  1072.0 9.3 reshape.74
  1081.3 0.0 copy-start.4
  1081.3 8.4 copy.58
  1089.7 0.0 copy-done.4
  1089.8 0.8 fusion.1
  (2 shorter events, 0.0 us)
Async XLA Ops:
  7.2 961.2 %copy-start = (bf16[3,2560,112]{1,2,0:T(8,128)(2,1)S(1)}, bf16[3,2560,112]{1,2,0:T(8,128)(2,1)}, u32[]{:S(2)}) copy-start(bf16[3,2560,112]{1,2,0:T(8,128)(2,1)} %param.12) | copy-start | bytes 5160964
  7.2 341.3 %all-gather.3.cloned.1.call-start = ((), (), s32[]{:S(2)}) async-start(), calls=%async_computation.3 | async-start | bytes 5591040 | tf_op jit(solution)/shard_map/all_gather | solution.py:51
  12.7 955.7 %all-gather.5.cloned.1.call-start = ((), (), s32[]{:S(2)}) async-start(), calls=%async_computation.4 | async-start | bytes 1996800 | tf_op jit(solution)/shard_map/all_gather | solution.py:57
  648.2 9.2 copy-start.1
  993.5 66.2 %copy-start.3 = (bf16[1,1024,256]{2,1,0:T(8,128)(2,1)S(1)}, bf16[1,1024,256]{2,1,0:T(8,128)(2,1)}, u32[]{:S(2)}) copy-start(bf16[1,1024,256]{2,1,0:T(8,128)(2,1)} %param.14) | copy-start | bytes 1572868
  993.5 66.2 %copy-start.5 = (bf16[1,64,256]{2,1,0:T(8,128)(2,1)S(1)}, bf16[1,64,256]{2,1,0:T(8,128)(2,1)}, u32[]{:S(2)}) copy-start(bf16[1,64,256]{2,1,0:T(8,128)(2,1)} %param.13) | copy-start | bytes 98308
  993.5 66.9 %copy-start.2 = (bf16[1,1024,256]{2,1,0:T(8,128)(2,1)S(1)}, bf16[1,1024,256]{2,1,0:T(8,128)(2,1)}, u32[]{:S(2)}) copy-start(bf16[1,1024,256]{2,1,0:T(8,128)(2,1)} %param.15) | copy-start | bytes 1572868
  1002.4 69.6 %all-to-all-start.2 = ((bf16[8,2,2688]{2,1,0:T(2,128)(2,1)}), bf16[8,2,2688]{2,1,0:T(2,128)(2,1)S(1)}, u32[]{:S(2)}, u32[]{:S(2)}) async-start(bf16[8,2,2688]{2,1,0:T(2,128)(2,1)} %reshape.73), calls=%async_computation.2 | async-start | bytes 172032 | tf_op jit(solution)/shard_map/all_to_all | solution.py:62
  1081.3 8.5 copy-start.4
Sparse Core Ops, SparseCore 0:
  12.8 335.5 all-gather.2
  662.7 305.6 all-gather.4
where the time goes:
time: 1100 us
  waiting for transfers between devices  652 us (59%)
  blocking collectives  308 us (28%)
  starting transfers between devices  57.4 us (5%)
  local copies, waits for them, and re-layouts  52.7 us (5%)
  between operations  14.2 us (1%)
    all_gather x1, waiting for transfers between devices, shards(): everyone = lax.all_gather(outgoing, ('req', 'head'), axis=2, tiled=True)  336 us
    all_gather x1, waiting for transfers between devices, shards(): lax.all_gather(hidden, ('req', 'head'), axis=2, tiled=True)  306 us
    all_to_all x1, blocking collectives, shards(): lax.all_to_all(everyone, 'exp', split_axis=0, concat_axis=3, tiled=True)  291 us
    all_to_all x1, starting transfers between devices, shards(): lax.all_to_all(lax.all_to_all(result, ('req', 'head'), split_axis=1, conc...  57.3 us
  transfers between devices with their start and end apart: 3, of which 3 were waited for; matrix products, arithmetic and copies ran while one was open for 0% of the time, Pallas kernels for 0%

commit v1 on v0

v1 whole, which is shorter than its diff:
```python
import functools
import math

import jax
import jax.numpy as jnp
from jax import lax
from jax.experimental import pallas as pl
from jax.experimental.pallas import tpu as pltpu
from jax.sharding import PartitionSpec as P

BF = jnp.bfloat16
F32 = jnp.float32
I32 = jnp.int32
NT = (((1,), (1,)), ((), ()))


def iota(shape, dim):
    return lax.broadcasted_iota(I32, shape, dim)


def onehot(match):
    return jnp.where(match, 1.0, 0.0).astype(BF)


def dot(a, b):
    return jnp.dot(a, b, preferred_element_type=F32)


def attend(q, k, v):
    scores = lax.dot_general(q, k, NT, preferred_element_type=F32) * (1.0 / math.sqrt(q.shape[1]))
    weights = jnp.exp(scores - jnp.max(scores, axis=1, keepdims=True))
    total = jnp.sum(weights, axis=1, keepdims=True)
    return (dot(weights.astype(BF), v) / total).astype(BF)


def kernel(
    n,
    ids_ref, wt_ref, x_ref, q_ref, k_hbm, v_hbm, up_hbm, down_hbm,
    out_ref, ctx_ref,
    k_ref, v_ref, down_ref, up_ref, upcat_ref, wd_ref,
    tok_ref, named_ref, send1_ref, recv1_ref, xg_ref, part_ref, partin_ref,
    hg_ref, acc_ref, r1s_ref, r1r_ref, r2s_ref, r2r_ref,
    loc_sem, up_s, up_r, s1_s, s1_r, s2_s, s2_r, s3_s, s3_r, pt_s, pt_r,
    hz_s, hz_r, hg_s, hg_r, ho_s, ho_r, r1_s, r1_r, r2_s, r2_r,
):
    toks, width = x_ref.shape
    dq = 2 * width
    half = send1_ref.shape[1]
    fs = up_ref.shape[2]
    dn = down_ref.shape[2]
    g2 = 2 * n
    unit = 12 * n
    rows = 2 * n * n * n
    plane = n * n
    column = 2 * plane

    req, zl, ex = lax.axis_index("req"), lax.axis_index("head"), lax.axis_index("exp")
    y, x = req // n, req % n
    zh, c = ex // 2, ex % 2
    g = x * (1 - c) + y * c
    o = y * (1 - c) + x * c

    def rid(g_, o_, c_):
        return (o_ * (1 - c_) + g_ * c_) * n + g_ * (1 - c_) + o_ * c_

    def dev(r_, zl_, ex_):
        return {"req": r_, "head": zl_, "exp": ex_}

    def remote(src, dst, ss, rs, where):
        return pltpu.make_async_remote_copy(
            src_ref=src, dst_ref=dst, send_sem=ss, recv_sem=rs,
            device_id=where, device_id_type=pl.DeviceIdType.MESH,
        )

    def add(v, d, m=n):
        return (v + d) % m

    sends = []

    load_down = pltpu.make_async_copy(down_hbm, down_ref, loc_sem.at[0])
    load_k = pltpu.make_async_copy(k_hbm, k_ref, loc_sem.at[1])
    load_v = pltpu.make_async_copy(v_hbm, v_ref, loc_sem.at[2])
    load_up = pltpu.make_async_copy(up_hbm.at[:, :, pl.ds(g * dq, dq)], up_ref.at[g], loc_sem.at[3])
    load_up.start()
    load_k.start()
    load_v.start()
    load_down.start()

    barrier = pltpu.get_barrier_semaphore()

    def greet(where):
        pl.semaphore_signal(barrier, inc=1, device_id=where, device_id_type=pl.DeviceIdType.MESH)

    def greet_plane(d, carry):
        greet(dev(add(req, d, plane), zl, ex))
        return carry

    def greet_column(d, carry):
        m = add(zl * g2 + ex, d, column)
        greet(dev(req, m // g2, m % g2))
        return carry

    lax.fori_loop(1, plane, greet_plane, 0)
    lax.fori_loop(1, column, greet_column, 0)

    targets = []
    for dt in range(2):
        t = (c + dt) % 2
        g_t = x * (1 - t) + y * t
        o_t = y * (1 - t) + x * t
        for dz in range(n):
            zt = add(zh, dz)
            targets.append((t, g_t, zt, dev(rid(zh, o_t, t), zl, zt * 2 + t), dt == 0 and dz == 0))
    home = g == zh
    for t, g_t, zt, where, own in targets:
        if own:
            @pl.when(jnp.logical_not(home))
            def _():
                greet(where)
        else:
            greet(where)
    for dt in range(2):
        cs = (c + dt) % 2
        for dg in range(n):
            gs = add(g, dg)
            where = dev(rid(gs, o, c), zl, g * 2 + cs)
            if dt == 0 and dg == 0:
                @pl.when(jnp.logical_not(home))
                def _():
                    greet(where)
            else:
                greet(where)

    lanes = g2 * 16
    lane = iota((1, lanes), 1)
    low = lane % 8
    lane_expert = jnp.where(low < 6, (lane // 16) * 3 + low // 2, -1)
    ids = ids_ref[...]
    wts = wt_ref[...]
    named = jnp.zeros((toks, lanes), F32)
    weight = jnp.zeros((toks, lanes), F32)
    for kk in range(3):
        hit = ids[:, kk:kk + 1] == lane_expert
        named = named + jnp.where(hit, 1.0, 0.0)
        weight = weight + jnp.where(hit, wts[:, kk:kk + 1], 0.0)
    named_ref[...] = jnp.zeros_like(named_ref)
    named_ref[0, 0:toks, :] = named
    named_ref[1, 0:toks, :] = weight
    tok_ref[...] = jnp.zeros_like(tok_ref)
    tok_ref[0:toks, 0:width] = x_ref[...]
    named = named_ref[0]
    tri = onehot(iota((16, 16), 0) > iota((16, 16), 1))
    before = dot(tri, named.astype(BF))
    pick = jnp.where(before == (lane % 2).astype(F32), named, 0.0)
    comb = pick * named_ref[1]
    spread = dot(pick.T.astype(BF), tok_ref[...])
    upper = (iota((lanes, 1), 0) % 16) >= 8
    send1_ref[...] = jnp.where(upper, spread[:, half:], spread[:, :half]).astype(BF)

    @pl.when(home)
    def _():
        pl.semaphore_wait(barrier, plane - 1 + column - 1 + 2 * (2 * n - 1))

    @pl.when(jnp.logical_not(home))
    def _():
        pl.semaphore_wait(barrier, plane - 1 + column - 1 + 2 * (2 * n))

    firsts = []
    for at, (t, g_t, zt, where, own) in enumerate(targets):
        src = send1_ref.at[pl.ds((zt * 2 + t) * 16, 16), :]
        place = c * n + g_t
        dst = recv1_ref.at[pl.ds(place * 16, 16), :]
        cp = remote(src, dst, s1_s.at[at], s1_r.at[place], where)
        firsts.append(cp)
        if own:
            @pl.when(home)
            def _():
                pltpu.make_async_copy(src, dst, s1_r.at[place]).start()

            @pl.when(jnp.logical_not(home))
            def _():
                cp.start()
        else:
            cp.start()
            sends.append(cp)

    ups = []
    for d in range(1, n):
        p = add(g, d)
        cp = remote(
            up_hbm.at[:, :, pl.ds(p * dq, dq)], up_ref.at[g], up_s.at[d], up_r.at[d],
            dev(rid(p, o, c), zl, ex),
        )
        cp.start()
        ups.append(cp)
        sends.append(cp)

    load_k.wait()
    load_v.wait()
    ctx_ref[...] = attend(q_ref[...], k_ref[...], v_ref[...])

    for i in range(2 * n):
        ref = recv1_ref.at[pl.ds(i * 16, 16), :]
        pltpu.make_async_copy(ref, ref, s1_r.at[i]).wait()

    ru = iota((unit, 2 * n * 16), 0)
    second = jnp.where(ru >= 6 * n, 1, 0)
    rest = ru - 6 * n * second
    origin = (second * n + (rest % g2) // 2) * 16 + (rest // g2) * 2 + rest % 2
    col = iota((unit, 2 * n * 16), 1)
    got = recv1_ref[...]
    left = dot(onehot(col == origin), got).astype(BF)
    right = dot(onehot(col == origin + 8), got).astype(BF)
    xg_ref[o, zl, :, 0:half] = left
    xg_ref[o, zl, :, half:width] = right[:, 0:width - half]

    def around(piece, ss, rs):
        for d in range(1, n):
            cp = remote(piece, piece, ss.at[d], rs.at[d], dev(rid(g, add(o, d), c), zl, ex))
            cp.start()
            sends.append(cp)

    for d in (list(range(1, n))):
        own = xg_ref.at[o, zl]
        cp = remote(own, own, s2_s.at[d], s2_r.at[d], dev(req, add(zl, d), ex))
        cp.start()
        sends.append(cp)
    around(xg_ref.at[o, zl], s3_s.at[0], s3_r.at[0])

    load_down.wait()
    wd_ref[...] = jnp.zeros_like(wd_ref)

    def spread_down(i, carry):
        for k in range(3):
            both = down_ref[k, pl.ds(pl.multiple_of(i * 2 * fs, 16), 2 * fs), :].astype(F32)
            for side in range(2):
                piece = both[side * fs:(side + 1) * fs]
                parts = [piece]
                if k:
                    parts = [jnp.zeros((k * fs, dn), F32)] + parts
                parts.append(jnp.zeros((128 - (k + 1) * fs, dn), F32))
                wd_ref[i, side * 128:(side + 1) * 128, k * 128:k * 128 + dn] = jnp.concatenate(
                    parts, axis=0).astype(BF)
        return carry

    lax.fori_loop(0, n * n * n // 2, spread_down, 0)

    for dz in range(1, n):
        piece = xg_ref.at[o, add(zl, n - dz)]
        pltpu.make_async_copy(piece, piece, s2_r.at[dz]).wait()
        around(piece, s3_s.at[dz], s3_r.at[dz])

    def fix_up(p):
        for h in range(2):
            parts = [up_ref[p, k, :, h * width:(h + 1) * width].astype(F32) for k in range(3)]
            parts.append(jnp.zeros((128 - 3 * fs, width), F32))
            upcat_ref[p, h * 128:(h + 1) * 128, :] = jnp.concatenate(parts, axis=0).astype(BF)

    load_up.wait()
    fix_up(g)
    for d in range(1, n):
        p = add(g, n - d)
        pltpu.make_async_copy(up_ref.at[p], up_ref.at[p], up_r.at[d]).wait()
        fix_up(p)

    band = iota((1, 1, 128), 2)
    for d in range(n):
        os = add(o, n - d)
        if d:
            for dz in range(n):
                piece = xg_ref.at[os, add(zl, n - dz)]
                pltpu.make_async_copy(piece, piece, s3_r.at[dz, d]).wait()

        def products(p, carry):
            a = xg_ref[os].reshape(n * unit, width)
            r = lax.dot_general(a, upcat_ref[p], NT, preferred_element_type=F32)
            r = r.reshape(n, unit, 256)
            total = jnp.zeros((n, g2, 128), F32)
            for h in range(2):
                rk = [
                    r[:, (3 * h + k) * g2:(3 * h + k + 1) * g2, h * 128:(h + 1) * 128]
                    for k in range(3)
                ]
                total = total + jnp.where(
                    band < fs, rk[0], jnp.where(band < 2 * fs, rk[1], rk[2]))
            part_ref[p, os] = total.reshape(n * g2, 128)
            return carry

        lax.fori_loop(0, n, products, 0)

    for d in range(1, n):
        p = add(g, d)
        cp = remote(part_ref.at[p], partin_ref.at[d - 1], pt_s.at[d], pt_r.at[d], dev(rid(p, o, c), zl, ex))
        cp.start()
        sends.append(cp)
    raised = part_ref[g]
    for d in range(1, n):
        ref = partin_ref.at[d - 1]
        pltpu.make_async_copy(ref, ref, pt_r.at[d]).wait()
        raised = raised + partin_ref[d - 1]
    raised = raised.reshape(rows, 128)
    hidden = (raised / (1.0 + jnp.exp(-raised))).astype(BF)
    rn = iota((rows, rows), 0)
    src = ((rn // (g2 * n)) * n + (rn % g2) // 2) * g2 + ((rn // g2) % n) * 2 + rn % 2
    hidden = dot(onehot(iota((rows, rows), 1) == src), hidden).astype(BF)

    def hpiece(g_, o_, z_):
        return hg_ref.at[g_, o_, :, pl.ds(z_ * 128, 128)]

    hg_ref[g, o, :, pl.ds(pl.multiple_of(zl * 128, 128), 128)] = hidden

    def hgroup(dz):
        piece = hpiece(g, o, add(zl, n - dz))
        for d in range(1, n):
            cp = remote(piece, piece, hg_s.at[dz, d], hg_r.at[dz, d], dev(rid(add(g, d), o, c), zl, ex))
            cp.start()
            sends.append(cp)

    def hother(dg):
        piece = hg_ref.at[add(g, n - dg), o]
        for d in range(1, n):
            cp = remote(piece, piece, ho_s.at[dg, d], ho_r.at[dg, d], dev(rid(g, add(o, d), c), zl, ex))
            cp.start()
            sends.append(cp)

    own = hpiece(g, o, zl)
    for d in range(1, n):
        cp = remote(own, own, hz_s.at[d], hz_r.at[d], dev(req, add(zl, d), ex))
        cp.start()
        sends.append(cp)
    hgroup(0)
    for dz in range(1, n):
        piece = hpiece(g, o, add(zl, n - dz))
        pltpu.make_async_copy(piece, piece, hz_r.at[dz]).wait()
        hgroup(dz)
    hother(0)

    def lower(g_, o_):
        r_ = rid(g_, o_, c)
        w = wd_ref[pl.ds(r_ * (n // 2), n // 2)].reshape(n * 128, 384)
        acc_ref[...] += dot(hg_ref[g_, o_], w)

    acc_ref[...] = jnp.zeros_like(acc_ref)
    lower(g, o)
    for dg in range(1, n):
        gs = add(g, n - dg)
        for dz in range(n):
            piece = hpiece(gs, o, add(zl, n - dz))
            pltpu.make_async_copy(piece, piece, hg_r.at[dz, dg]).wait()
        hother(dg)
        lower(gs, o)
    for dg in range(n):
        gs = add(g, n - dg)
        for d in range(1, n):
            os = add(o, n - d)
            piece = hg_ref.at[gs, os]
            pltpu.make_async_copy(piece, piece, ho_r.at[dg, d]).wait()
            lower(gs, os)

    acc = acc_ref[...].reshape(plane, g2, 384)
    if g2 < 8:
        acc = jnp.concatenate([acc, jnp.zeros((plane, 8 - g2, 384), F32)], axis=1)
    lower_rows = jnp.concatenate([acc[:, :, 256:384], jnp.zeros((plane, 8, 128), F32)], axis=2)
    r1s_ref[...] = jnp.concatenate([acc[:, :, 0:256], lower_rows], axis=1).astype(BF)
    spot = o * n + g

    def r1_send(d, carry):
        i = add(spot, d, plane)
        remote(
            r1s_ref.at[i], r1r_ref.at[req], r1_s.at[0], r1_r.at[0],
            dev(rid(i % n, i // n, c), zl, ex),
        ).start()
        return carry

    lax.fori_loop(1, plane, r1_send, 0)
    r1r_ref[req] = r1s_ref[spot]

    hn = n // 2
    mr = hn * 8
    rr = iota((column * mr, plane * 16), 0)
    m = rr // mr
    xi = (rr % mr) // 8
    k2 = (rr % 8) // 2
    e2 = m % g2
    srcx = (e2 // 2) * n + (e2 % 2) * hn + xi
    origin = srcx * 16 + (k2 // 2) * 8 + (m // g2) * 2 + rr % 2
    same = iota((column * mr, plane * 16), 1) == origin
    take_a = onehot(jnp.logical_and(same, jnp.logical_or(k2 == 0, k2 == 2)))
    take_b = onehot(jnp.logical_and(same, k2 == 1))

    others = r1r_ref.at[pl.ds(0, plane - 1)]
    pltpu.make_async_copy(others, others, r1_r.at[0]).wait()
    got = r1r_ref[...].reshape(plane * 16, 256)
    r2s_ref[...] = (dot(take_a, got[:, 0:128]) + dot(take_b, got[:, 128:256])).astype(BF).reshape(
        column, mr, 128)
    spot2 = zl * g2 + ex

    def r2_dst():
        return r2r_ref.at[pl.ds(ex * mr, mr), pl.ds(zl * 128, 128)]

    def r2_send(d, carry):
        i = add(spot2, d, column)
        remote(r2s_ref.at[i], r2_dst(), r2_s.at[0], r2_r.at[0], dev(req, i // g2, i % g2)).start()
        return carry

    lax.fori_loop(1, column, r2_send, 0)
    keep = pltpu.make_async_copy(r2s_ref.at[spot2], r2_dst(), loc_sem.at[4])
    keep.start()
    keep.wait()
    others = r2s_ref.at[pl.ds(0, column - 1)]
    pltpu.make_async_copy(others, others, r2_r.at[0]).wait()

    cut = lane % 16
    both = []
    for xi_at in range(hn):
        both.append(jnp.where(cut // 8 == xi_at, comb, 0.0))
    both = jnp.concatenate(both, axis=0)
    if mr < 16:
        both = both.reshape(16 * hn, g2, 16)[:, :, 0:mr].reshape(16 * hn, g2 * mr)
    p0 = both.astype(BF)
    left_over = both - p0.astype(F32)
    p1 = left_over.astype(BF)
    p2 = (left_over - p1.astype(F32)).astype(BF)
    got = r2r_ref[...]
    sums = dot(p0, got) + (dot(p1, got) + dot(p2, got))
    pieces = []
    for xi_at in range(hn):
        for z in range(n):
            pieces.append(sums[xi_at * 16:xi_at * 16 + toks, z * 128:z * 128 + dn])
    total = jnp.concatenate(pieces, axis=1)
    out_ref[...] = (x_ref[...].astype(F32) + total).astype(BF)

    for cp in sends:
        cp.wait_send()

    @pl.when(jnp.logical_not(home))
    def _():
        firsts[0].wait_send()
    others = r1s_ref.at[pl.ds(0, plane - 1)]
    pltpu.make_async_copy(others, others, r1_s.at[0]).wait()
    others = r2s_ref.at[pl.ds(0, column - 1)]
    pltpu.make_async_copy(others, others, r2_s.at[0]).wait()


def shards(moe_input, route_ids, route_weight, w_up, w_down, queries, keys, values):
    n = lax.axis_size("head")
    toks, width = moe_input.shape
    fs = w_up.shape[1]
    dn = w_down.shape[2]
    ffh = w_down.shape[1]
    heads, hd = queries.shape[1:]
    length = keys.shape[1]
    dq = 2 * width
    half = -(-width // 256) * 128
    rows = 2 * n * n * n
    plane, column = n * n, 2 * n * n
    mr = (n // 2) * 8
    vm = pl.BlockSpec(memory_space=pltpu.VMEM)
    hbm = pl.BlockSpec(memory_space=pl.ANY)
    dma = pltpu.SemaphoreType.DMA
    moe, ctx = pl.pallas_call(
        functools.partial(kernel, n),
        out_shape=(
            jax.ShapeDtypeStruct((toks, width), BF),
            jax.ShapeDtypeStruct((heads, hd), BF),
        ),
        in_specs=[vm, vm, vm, vm, hbm, hbm, hbm, hbm],
        out_specs=(vm, vm),
        scratch_shapes=[
            pltpu.VMEM((length, hd), BF),
            pltpu.VMEM((length, hd), BF),
            pltpu.VMEM((3, ffh, dn), BF),
            pltpu.VMEM((n, 3, fs, dq), BF),
            pltpu.VMEM((n, 256, width), BF),
            pltpu.VMEM((n * n * n // 2, 256, 384), BF),
            pltpu.VMEM((16, 2 * half), BF),
            pltpu.VMEM((2, 16, 32 * n), F32),
            pltpu.VMEM((32 * n, half), BF),
            pltpu.VMEM((32 * n, half), BF),
            pltpu.VMEM((n, n, 12 * n, width), BF),
            pltpu.VMEM((n, n, 2 * n * n, 128), F32),
            pltpu.VMEM((n - 1, n, 2 * n * n, 128), F32),
            pltpu.VMEM((n, n, rows, n * 128), BF),
            pltpu.VMEM((rows, 384), F32),
            pltpu.VMEM((plane, 16, 256), BF),
            pltpu.VMEM((plane, 16, 256), BF),
            pltpu.VMEM((column, mr, 128), BF),
            pltpu.VMEM((2 * n * mr, n * 128), BF),
            dma((5,)),
            dma((n,)), dma((n,)),
            dma((2 * n,)), dma((2 * n,)),
            dma((n,)), dma((n,)),
            dma((n, n)), dma((n, n)),
            dma((n,)), dma((n,)),
            dma((n,)), dma((n,)),
            dma((n, n)), dma((n, n)),
            dma((n, n)), dma((n, n)),
            dma((1,)), dma((1,)),
            dma((1,)), dma((1,)),
        ],
        compiler_params=pltpu.CompilerParams(
            collective_id=0, has_side_effects=True, vmem_limit_bytes=48 * 1024 * 1024
        ),
        cost_estimate=pl.CostEstimate(flops=10**9, bytes_accessed=10**7, transcendentals=10**5),
        name="decode",
    )(route_ids, route_weight, moe_input, queries[0], keys[0], values[0], w_up, w_down)
    return (moe, ctx[None])


def solution(mesh):
    placed = (
        P(("req", "head"), "exp"),
        P(("req", "head"), None),
        P(("req", "head"), None),
        P("exp", ("req", "head"), None),
        P("exp", None, ("req", "head")),
        P(("req", "head", "exp"), None, None),
        P(("req", "head", "exp"), None, None),
        P(("req", "head", "exp"), None, None),
    )
    return jax.shard_map(
        shards,
        mesh=mesh,
        in_specs=placed,
        out_specs=(P(("req", "head"), "exp"), P(("req", "head", "exp"), None, None)),
        check_vma=False,
    )
```

time: 1100 us -> 101 us (0.09)
  waiting for transfers between devices: 652 us -> 0 us
  blocking collectives: 308 us -> 0 us
  Pallas kernels: 0 us -> 93.4 us
  starting transfers between devices: 57.4 us -> 0 us
  local copies, waits for them, and re-layouts: 52.7 us -> 7.12 us
  between operations: 14.2 us -> 0.69 us
    all_gather x2 -> x0, waiting for transfers between devices: 641 us -> none  [the longest x1 336 us: shards(): everyone = lax.all_gather(outgoing, ('req', 'head'), axis=2, tiled=True)]
    all_to_all x2 -> x0, blocking collectives: 308 us -> none  [the longest x1 291 us: shards(): lax.all_to_all(everyone, 'exp', split_axis=0, concat_axis=3, tiled=True)]
    pallas_call x0 -> x1, Pallas kernels: none -> 93.4 us  [shards(): pl.pallas_call(functools.partial(kernel, n), out_shape=(jax.ShapeDtypeStr...]
    all_to_all x1 -> x0, starting transfers between devices: 57.3 us -> none  [shards(): lax.all_to_all(lax.all_to_all(result, ('req', 'head'), split_axis=1, conc...]
    all_to_all x3 -> x0, local copies, waits for them, and re-layouts: 19.9 us -> none  [the longest x1 8.44 us: shards(): lax.all_to_all(lax.all_to_all(result, ('req', 'head'), split_axis=1, conc...]
    unnamed x15, local copies, waits for them, and re-layouts: 18.9 us -> 7.12 us
  transfers between devices with their start and end apart: 3 -> 0, of which waited for: 3 -> 0; matrix products, arithmetic and copies ran while one was open for 0% -> 0% of each run, Pallas kernels for 0% -> 0%
where the time goes in v1:
time: 101 us
  Pallas kernels  93.4 us (92%)
  local copies, waits for them, and re-layouts  7.12 us (7%)
    pallas_call x1, Pallas kernels, shards(): pl.pallas_call(functools.partial(kernel, n), out_shape=(jax.ShapeDtypeStr...  93.4 us
    unnamed x15, local copies, waits for them, and re-layouts  7.12 us

profile of v1, /device:TPU:1, one launch (start us, length us, event | category | flops | bytes accessed | tf_op | source)
XLA Modules:
  0.0 101.2 jit_solution(10215786538551293790)
XLA Ops:
  0.6 0.8 copy.10.ids_ref
  1.4 0.8 copy.11.wt_ref
  2.2 0.0 copy-start.1
  2.2 0.0 copy-start.2
  2.2 0.0 copy-start.3
  2.2 0.0 copy-start.4
  2.2 2.9 %copy.12.down_hbm = bf16[3,2560,112]{2,1,0:T(8,128)(2,1)S(1)} copy(bf16[3,2560,112]{1,2,0:T(8,128)(2,1)} %param.12) | data formatting | bytes 3440640 | tf_op args[4]
  5.1 0.0 copy-done.1
  5.1 0.0 copy-done.2
  5.1 0.0 copy-done.3
  5.1 0.0 copy-done.4
  5.1 0.0 copy-start
  5.1 1.5 %copy-done = bf16[3,40,7168]{2,1,0:T(8,128)(2,1)S(1)} copy-done((bf16[3,40,7168]{2,1,0:T(8,128)(2,1)S(1)}, bf16[3,40,7168]{2,1,0:T(8,128)(2,1)}, u32[]{:S(2)}) %copy-start) | copy-done | bytes 1720344
  6.6 93.4 %decode.1 = (bf16[12,896]{1,0:T(8,128)(2,1)S(1)}, bf16[64,256]{1,0:T(8,128)(2,1)S(1)}) custom-call(s32[12,3]{1,0:T(8,128)S(1)} %copy.10.ids_ref, f32[12,3]{1,0:T(8,128)S(1)} %copy.11.wt_ref, bf16[12,896]{1,0:T(8,128)(2,1)S(1)} %copy-done.4, bf16[64,256]{1,0:T(8,128)(2,1)S(1)} %bitcast.6, bf16[1024,256]{1,0:T(8,128)(2,1)S(1)} %bitcast.4, ...), custom_call_target="tpu_custom_call" | custom-call | flops 1000000000 | bytes 10000000 | tf_op jit(solution)/shard_map/decode/pallas_call | solution.py:461
  99.9 0.6 copy.15
  100.6 0.6 copy.16
Async XLA Ops:
  2.2 2.9 %copy-start.1 = (bf16[1,1024,256]{2,1,0:T(8,128)(2,1)S(1)}, bf16[1,1024,256]{2,1,0:T(8,128)(2,1)}, u32[]{:S(2)}) copy-start(bf16[1,1024,256]{2,1,0:T(8,128)(2,1)} %param.14) | copy-start | bytes 1572868
  2.2 2.9 %copy-start.2 = (bf16[1,1024,256]{2,1,0:T(8,128)(2,1)S(1)}, bf16[1,1024,256]{2,1,0:T(8,128)(2,1)}, u32[]{:S(2)}) copy-start(bf16[1,1024,256]{2,1,0:T(8,128)(2,1)} %param.15) | copy-start | bytes 1572868
  2.2 2.9 %copy-start.3 = (bf16[1,64,256]{2,1,0:T(8,128)(2,1)S(1)}, bf16[1,64,256]{2,1,0:T(8,128)(2,1)}, u32[]{:S(2)}) copy-start(bf16[1,64,256]{2,1,0:T(8,128)(2,1)} %param.13) | copy-start | bytes 98308
  2.2 2.9 %copy-start.4 = (bf16[12,896]{1,0:T(8,128)(2,1)S(1)}, bf16[12,896]{1,0:T(8,128)(2,1)}, u32[]{:S(2)}) copy-start(bf16[12,896]{1,0:T(8,128)(2,1)} %x_ref.1) | copy-start | bytes 64516
  5.1 1.5 %copy-start = (bf16[3,40,7168]{2,1,0:T(8,128)(2,1)S(1)}, bf16[3,40,7168]{2,1,0:T(8,128)(2,1)}, u32[]{:S(2)}) copy-start(bf16[3,40,7168]{2,1,0:T(8,128)(2,1)} %up_hbm.1) | copy-start | bytes 5160964

commit v2 on v0

v2 whole, which is shorter than its diff:
```python
import functools
import math

import jax
import jax.numpy as jnp
from jax import lax
from jax.experimental import pallas as pl
from jax.experimental.pallas import tpu as pltpu
from jax.sharding import PartitionSpec as P

BF = jnp.bfloat16
F32 = jnp.float32
I32 = jnp.int32
NT = (((1,), (1,)), ((), ()))


def iota(shape, dim):
    return lax.broadcasted_iota(I32, shape, dim)


def onehot(match):
    return jnp.where(match, 1.0, 0.0).astype(BF)


def dot(a, b):
    return jnp.dot(a, b, preferred_element_type=F32)


def attend(q, k, v):
    scores = lax.dot_general(q, k, NT, preferred_element_type=F32) * (1.0 / math.sqrt(q.shape[1]))
    weights = jnp.exp(scores - jnp.max(scores, axis=1, keepdims=True))
    total = jnp.sum(weights, axis=1, keepdims=True)
    return (dot(weights.astype(BF), v) / total).astype(BF)


def kernel(
    n, nz,
    ids_ref, wt_ref, x_hbm, q_hbm, k_hbm, v_hbm, up_hbm, down_hbm,
    out_ref, ctx_ref,
    x_ref, q_ref, k_ref, v_ref, down_ref, up_ref, upcat_ref, wd_ref,
    tok_ref, ids_pad, send1_ref, recv1_ref, xg_ref, part_ref, partin_ref,
    hg_ref, acc_ref, r1s_ref, r1r_ref, r2r_ref,
    loc_sem, up_s, up_r, s1_s, s1_r, s2_s, s2_r, s3_s, s3_r,
    pt_s, pt_r, hz_s, hz_r, hg_s, hg_r, ho_s, ho_r,
    r1_s, r1_r, r2_s, r2_r,
):
    toks, width = x_ref.shape
    dq = 2 * width
    chunks = width // 128
    fs = up_ref.shape[2]
    dn = down_ref.shape[1]
    g2 = 2 * n
    unit = 12 * n
    rows = 2 * n * n * nz
    plane = n * n
    column = g2 * nz
    srcs = plane * nz
    hops = (2, 1, 3) if n == 4 else (1,)

    req, zl, ex = lax.axis_index("req"), lax.axis_index("head"), lax.axis_index("exp")
    y, x = req // n, req % n
    zh, c = ex // 2, ex % 2
    g = x * (1 - c) + y * c
    o = y * (1 - c) + x * c

    def rid(g_, o_, c_):
        return (o_ * (1 - c_) + g_ * c_) * n + g_ * (1 - c_) + o_ * c_

    def dev(r_, zl_, ex_):
        return {"req": r_, "head": zl_, "exp": ex_}

    def remote(src, dst, ss, rs, where):
        return pltpu.make_async_remote_copy(
            src_ref=src, dst_ref=dst, send_sem=ss, recv_sem=rs,
            device_id=where, device_id_type=pl.DeviceIdType.MESH,
        )

    def arrived(ref, sem):
        pltpu.make_async_copy(ref, ref, sem).wait()

    def add(v, d, m=n):
        return (v + d) % m

    sends = []

    def send(src, dst, ss, rs, where):
        cp = remote(src, dst, ss, rs, where)
        cp.start()
        sends.append(cp)

    def at_group(d):
        return dev(rid(add(g, d), o, c), zl, ex)

    def at_other(d):
        return dev(rid(g, add(o, d), c), zl, ex)

    def spread(block, where, ss, rs):
        for d in hops:
            send(block, block, ss.at[d], rs.at[d], where(d))

    loads = [
        (x_hbm, x_ref), (q_hbm, q_ref), (k_hbm, k_ref), (v_hbm, v_ref),
        (up_hbm.at[:, :, pl.ds(g * dq, dq)], up_ref.at[g]), (down_hbm, down_ref),
    ]
    loads = [pltpu.make_async_copy(a, b, loc_sem.at[i]) for i, (a, b) in enumerate(loads)]
    for cp in loads:
        cp.start()
    load_x, load_q, load_k, load_v, load_up, load_down = loads

    barrier = pltpu.get_barrier_semaphore()

    def greet(where):
        pl.semaphore_signal(barrier, inc=1, device_id=where, device_id_type=pl.DeviceIdType.MESH)

    def greet_plane(d, carry):
        greet(dev(add(req, d, plane), zl, ex))
        return carry

    def greet_column(d, carry):
        m = add(zl * g2 + ex, d, column)
        greet(dev(req, m // g2, m % g2))
        return carry

    lax.fori_loop(1, column, greet_column, 0)
    lax.fori_loop(1, plane, greet_plane, 0)

    targets = []
    for dz in hops + (0,):
        for dt in range(2):
            t = (c + dt) % 2
            g_t = x * (1 - t) + y * t
            o_t = y * (1 - t) + x * t
            zt = add(zh, dz)
            targets.append((t, g_t, zt, dev(rid(zh, o_t, t), zl, zt * 2 + t), dt == 0 and dz == 0))
    home = g == zh
    for t, g_t, zt, where, own in targets:
        if own:
            @pl.when(jnp.logical_not(home))
            def _():
                greet(where)
        else:
            greet(where)
    for dt in range(2):
        cs = (c + dt) % 2
        for dg in range(n):
            gs = add(g, dg)
            where = dev(rid(gs, o, c), zl, g * 2 + cs)
            if dt == 0 and dg == 0:
                @pl.when(jnp.logical_not(home))
                def _():
                    greet(where)
            else:
                greet(where)

    ids_pad[...] = jnp.zeros_like(ids_pad)
    ids_pad[0:3, 0:toks] = (ids_ref[...] + 1).astype(F32)
    hn = n // 2
    mr = hn * 8
    r128, c128 = iota((128, 128), 0), iota((128, 128), 1)
    tile = onehot(jnp.logical_and(c128 % 16 == r128, r128 < 16))
    tiled = dot(ids_pad[...].astype(BF), tile).astype(I32)
    tri = onehot(jnp.logical_and(r128 // 16 == c128 // 16, r128 % 16 < c128 % 16))
    grp = lax.broadcasted_iota(I32, (g2, 48, 128), 0)
    sub = lax.broadcasted_iota(I32, (g2, 48, 128), 1)
    lane = lax.broadcasted_iota(I32, (g2, 48, 128), 2)
    here = (lane // 16 == sub % 8).reshape(g2 * 48, 128)
    expert = (grp * 3 + sub // 16 + 1).reshape(g2 * 48, 128)
    slot = ((sub // 8) % 2).astype(F32).reshape(g2 * 48, 128)
    named = jnp.zeros((g2 * 48, 128), F32)
    for kk in range(3):
        hit = jnp.logical_and(here, tiled[kk:kk + 1, :] == expert)
        named = named + jnp.where(hit, 1.0, 0.0)
    before = dot(named.astype(BF), tri)
    pick = jnp.where(before == slot, named, 0.0).astype(BF)
    tok_ref[...] = jnp.zeros_like(tok_ref)
    load_x.wait()
    for ch in range(chunks):
        tok_ref[ch * 16:ch * 16 + toks, :] = x_ref[:, ch * 128:(ch + 1) * 128]
    send1_ref[...] = dot(pick, tok_ref[...]).astype(BF)

    @pl.when(home)
    def _():
        pl.semaphore_wait(barrier, plane - 1 + column - 1 + 2 * (2 * n - 1))

    @pl.when(jnp.logical_not(home))
    def _():
        pl.semaphore_wait(barrier, plane - 1 + column - 1 + 2 * (2 * n))

    first = None
    for at, (t, g_t, zt, where, own) in enumerate(targets):
        src = send1_ref.at[pl.ds((zt * 2 + t) * 48, 48), :]
        place = c * n + g_t
        dst = recv1_ref.at[pl.ds(place * 48, 48), :]
        cp = remote(src, dst, s1_s.at[at], s1_r.at[place], where)
        if own:
            first = cp

            @pl.when(home)
            def _():
                pltpu.make_async_copy(src, dst, s1_r.at[place]).start()

            @pl.when(jnp.logical_not(home))
            def _():
                cp.start()
        else:
            cp.start()
            sends.append(cp)

    for d in hops:
        send(
            up_hbm.at[:, :, pl.ds(add(g, d) * dq, dq)], up_ref.at[g],
            up_s.at[d], up_r.at[d], at_group(d),
        )

    load_q.wait()
    load_k.wait()
    load_v.wait()
    ctx_ref[...] = attend(q_ref[...], k_ref[...], v_ref[...])

    batch = min(16, srcs)

    def spread_down(i):
        for k in range(3):
            t = down_ref[k, :, i * batch * fs:(i + 1) * batch * fs].astype(F32).T
            for s in range(batch):
                parts = [t[s * fs:(s + 1) * fs]]
                if k:
                    parts = [jnp.zeros((k * fs, dn), F32)] + parts
                parts.append(jnp.zeros((128 - (k + 1) * fs, dn), F32))
                at = (i * batch + s) * 128
                wd_ref[at:at + 128, k * 128:k * 128 + dn] = jnp.concatenate(parts, axis=0).astype(BF)

    ru = lax.broadcasted_iota(I32, (chunks, unit, g2 * 48), 1)
    ch = lax.broadcasted_iota(I32, (chunks, unit, g2 * 48), 0)
    col = lax.broadcasted_iota(I32, (chunks, unit, g2 * 48), 2)
    second = jnp.where(ru >= 6 * n, 1, 0)
    rest = ru - 6 * n * second
    origin = (second * n + (rest % g2) // 2) * 48 + (rest // g2) * 16 + (rest % 2) * 8 + ch
    order = onehot(col == origin).reshape(chunks * unit, g2 * 48)
    for i in range(g2):
        arrived(recv1_ref.at[pl.ds(i * 48, 48), :], s1_r.at[i])
    placed = dot(order, recv1_ref[...]).astype(BF)
    for ch in range(chunks):
        xg_ref[o, zl, :, ch * 128:(ch + 1) * 128] = placed[ch * unit:(ch + 1) * unit]

    own = xg_ref.at[o, zl]
    for d in range(1, nz):
        send(own, own, s2_s.at[d], s2_r.at[d], dev(req, add(zl, d, nz), ex))

    def x_from(dz):
        return lambda d: xg_ref.at[add(o, d), add(zl, nz - dz, nz)]

    spread(own, at_other, s3_s.at[0], s3_r.at[0])
    load_down.wait()
    wd_ref[...] = jnp.zeros_like(wd_ref)
    batches = srcs // batch
    for i in range((batches + 1) // 2):
        spread_down(i)
    for dz in range(1, nz):
        block = x_from(dz)(0)
        arrived(block, s2_r.at[dz])
        spread(block, at_other, s3_s.at[dz], s3_r.at[dz])

    def fix_up(p):
        for h in range(2):
            parts = [up_ref[p, k, :, h * width:(h + 1) * width].astype(F32) for k in range(3)]
            parts.append(jnp.zeros((128 - 3 * fs, width), F32))
            upcat_ref[p, h * 128:(h + 1) * 128, :] = jnp.concatenate(parts, axis=0).astype(BF)

    load_up.wait()
    fix_up(g)
    for d in hops:
        p = add(g, n - d)
        arrived(up_ref.at[p], up_r.at[d])
        fix_up(p)

    band = iota((1, 1, 128), 2)

    def products(p, zs):
        a = xg_ref[:, zs].reshape(n * unit, width)
        r = lax.dot_general(a, upcat_ref[p], NT, preferred_element_type=F32)
        r = r.reshape(n, unit, 256)
        total = jnp.zeros((n, g2, 128), F32)
        for h in range(2):
            rk = [
                r[:, (3 * h + k) * g2:(3 * h + k + 1) * g2, h * 128:(h + 1) * 128]
                for k in range(3)
            ]
            total = total + jnp.where(band < fs, rk[0], jnp.where(band < 2 * fs, rk[1], rk[2]))
        part_ref[p, :, zs] = total

    for dz in range(nz):
        for d in hops:
            arrived(x_from(dz)(n - d), s3_r.at[dz, d])
        zs = add(zl, nz - dz, nz)
        for d in hops:
            p = add(g, d)
            products(p, zs)
            send(
                part_ref.at[p, :, zs], partin_ref.at[d - 1, :, zs],
                pt_s.at[dz, d], pt_r.at[dz, d], at_group(d),
            )
        products(g, zs)

    for i in range((batches + 1) // 2, batches):
        spread_down(i)

    raised = part_ref[g]
    for d in hops:
        for dz in range(nz):
            arrived(partin_ref.at[d - 1, :, add(zl, nz - dz, nz)], pt_r.at[dz, d])
        raised = raised + partin_ref[d - 1]
    raised = raised.reshape(rows, 128)
    hidden = (raised / (1.0 + jnp.exp(-raised))).astype(BF)

    def hpiece(g_, o_, z_):
        return hg_ref.at[g_, o_, :, pl.ds(pl.multiple_of(z_ * 128, 128), 128)]

    def g_from(dz):
        return lambda d: hpiece(add(g, d), o, add(zl, nz - dz, nz))

    def lower(g_, o_):
        r_ = rid(g_, o_, c)
        w = wd_ref[pl.ds(pl.multiple_of(r_ * (nz * 128), 128), nz * 128), :]
        acc_ref[...] += dot(hg_ref[g_, o_], w)

    hg_ref[g, o, :, pl.ds(pl.multiple_of(zl * 128, 128), 128)] = hidden
    own = hpiece(g, o, zl)
    for d in range(1, nz):
        send(own, own, hz_s.at[d], hz_r.at[d], dev(req, add(zl, d, nz), ex))
    spread(own, at_group, hg_s.at[0], hg_r.at[0])
    spread(own, at_other, ho_s.at[0, 0], ho_r.at[0, 0])
    acc_ref[...] = jnp.zeros_like(acc_ref)
    for dz in range(1, nz):
        piece = g_from(dz)(0)
        arrived(piece, hz_r.at[dz])
        spread(piece, at_group, hg_s.at[dz], hg_r.at[dz])
        spread(piece, at_other, ho_s.at[dz, 0], ho_r.at[dz, 0])
    for dz in range(nz):
        for dg in hops:
            piece = g_from(dz)(n - dg)
            arrived(piece, hg_r.at[dz, dg])
            spread(piece, at_other, ho_s.at[dz, dg], ho_r.at[dz, dg])
    for dg in range(n):
        lower(add(g, n - dg), o)
    for dg in (0,) + hops:
        gs = add(g, n - dg)
        for d in hops:
            os = add(o, n - d)
            for dz in range(nz):
                arrived(hpiece(gs, os, add(zl, nz - dz, nz)), ho_r.at[dz, dg, d])
            lower(gs, os)

    ro = iota((plane * nz * 8, rows), 0)
    co = iota((plane * nz * 8, rows), 1)
    low = ro % 8
    zt = (ro // 8) % nz
    spot_of = ro // (8 * nz)
    match = co - low % 2 == (((spot_of // n) * nz + zt) * n + spot_of % n) * 2
    picked = jnp.zeros((plane * nz * 8, 128), F32)
    for k in range(3):
        take = onehot(jnp.logical_and(match, low // 2 == k))
        picked = picked + dot(take, acc_ref[:, k * 128:(k + 1) * 128].astype(BF))
    r1s_ref[...] = picked.reshape(plane, nz, 8, 128).astype(BF)
    spot = o * n + g

    def r1_send(d, carry):
        i = add(spot, d, plane)
        remote(
            r1s_ref.at[i], r1r_ref.at[:, req], r1_s.at[0], r1_r.at[0],
            dev(rid(i % n, i // n, c), zl, ex),
        ).start()
        return carry

    lax.fori_loop(1, plane, r1_send, 0)
    keep = pltpu.make_async_copy(r1s_ref.at[spot], r1r_ref.at[:, req], loc_sem.at[6])
    keep.start()

    rw = iota((g2 * mr, 128), 0)
    low = rw % 8
    expert = jnp.where(low < 6, (rw // mr) * 3 + low // 2 + 1, -1)
    padded = ids_pad[...].astype(I32)
    weights = wt_ref[...]
    ids_pad[0:3, 0:toks] = weights
    weights = ids_pad[...]
    named = jnp.zeros((g2 * mr, 128), F32)
    weight = jnp.zeros((g2 * mr, 128), F32)
    for kk in range(3):
        hit = padded[kk:kk + 1, :] == expert
        named = named + jnp.where(hit, 1.0, 0.0)
        weight = weight + jnp.where(hit, weights[kk:kk + 1, :], 0.0)
    before = dot(named.astype(BF), onehot(r128 < c128))
    comb = jnp.where(before == (rw % 2).astype(F32), weight, 0.0)
    both = [jnp.where((rw % mr) // 8 == i, comb, 0.0).T[0:16] for i in range(hn)]
    both = jnp.concatenate(both, axis=0)
    p0 = both.astype(BF).astype(F32)
    p1 = (both - p0).astype(BF).astype(F32)
    parts = jnp.concatenate([p0, p1, both - p0 - p1], axis=0).astype(BF)

    keep.wait()
    arrived(r1s_ref.at[pl.ds(0, plane - 1)], r1_r.at[0])
    spot2 = zl * g2 + ex

    def r2_src(i):
        e2 = i % g2
        return r1r_ref.at[i // g2, pl.ds((e2 // 2) * n + (e2 % 2) * hn, hn)]

    def r2_send(d, carry):
        i = add(spot2, d, column)
        remote(
            r2_src(i), r2r_ref.at[spot2], r2_s.at[0], r2_r.at[0], dev(req, i // g2, i % g2)
        ).start()
        return carry

    lax.fori_loop(1, column, r2_send, 0)
    keep = pltpu.make_async_copy(r2_src(spot2), r2r_ref.at[spot2], loc_sem.at[7])
    keep.start()
    keep.wait()
    arrived(r2r_ref.at[pl.ds(0, column - 1)], r2_r.at[0])

    sums = [dot(parts, r2r_ref[z * g2:(z + 1) * g2].astype(F32).reshape(g2 * mr, 128).astype(BF)) for z in range(nz)]
    sums = jnp.concatenate(sums, axis=1)
    sums = sums[0:16 * hn] + (sums[16 * hn:32 * hn] + sums[32 * hn:48 * hn])
    pieces = []
    for i in range(hn):
        for z in range(nz):
            pieces.append(sums[i * 16:i * 16 + toks, z * 128:z * 128 + dn])
    total = jnp.concatenate(pieces, axis=1)
    out_ref[...] = (x_ref[...].astype(F32) + total).astype(BF)

    for cp in sends:
        cp.wait_send()

    @pl.when(jnp.logical_not(home))
    def _():
        first.wait_send()
    arrived(r1s_ref.at[pl.ds(0, plane - 1)], r1_s.at[0])
    arrived(r2r_ref.at[pl.ds(0, column - 1)], r2_s.at[0])


def shards(moe_input, route_ids, route_weight, w_up, w_down, queries, keys, values):
    nz = lax.axis_size("head")
    n = math.isqrt(lax.axis_size("req"))
    toks, width = moe_input.shape
    fs = w_up.shape[1]
    dn = w_down.shape[2]
    ffh = w_down.shape[1]
    heads, hd = queries.shape[1:]
    length = keys.shape[1]
    dq = 2 * width
    rows = 2 * n * n * nz
    plane = n * n
    vm = pl.BlockSpec(memory_space=pltpu.VMEM)
    hbm = pl.BlockSpec(memory_space=pl.ANY)
    dma = pltpu.SemaphoreType.DMA
    moe, ctx = pl.pallas_call(
        functools.partial(kernel, n, nz),
        out_shape=(
            jax.ShapeDtypeStruct((toks, width), BF),
            jax.ShapeDtypeStruct((heads, hd), BF),
        ),
        in_specs=[vm, vm, hbm, hbm, hbm, hbm, hbm, hbm],
        out_specs=(vm, vm),
        scratch_shapes=[
            pltpu.VMEM((toks, width), BF),
            pltpu.VMEM((heads, hd), BF),
            pltpu.VMEM((length, hd), BF),
            pltpu.VMEM((length, hd), BF),
            pltpu.VMEM((3, dn, ffh), BF),
            pltpu.VMEM((n, 3, fs, dq), BF),
            pltpu.VMEM((n, 256, width), BF),
            pltpu.VMEM((n * n * nz * 128, 384), BF),
            pltpu.VMEM((128, 128), BF),
            pltpu.VMEM((128, 128), F32),
            pltpu.VMEM((96 * n, 128), BF),
            pltpu.VMEM((96 * n, 128), BF),
            pltpu.VMEM((n, nz, 12 * n, width), BF),
            pltpu.VMEM((n, n, nz, 2 * n, 128), F32),
            pltpu.VMEM((n - 1, n, nz, 2 * n, 128), F32),
            pltpu.VMEM((n, n, rows, nz * 128), BF),
            pltpu.VMEM((rows, 384), F32),
            pltpu.VMEM((plane, nz, 8, 128), BF),
            pltpu.VMEM((nz, plane, 8, 128), BF),
            pltpu.VMEM((2 * n * nz, n // 2, 8, 128), BF),
            dma((8,)),
            dma((n,)), dma((n,)),
            dma((2 * n,)), dma((2 * n,)),
            dma((nz,)), dma((nz,)),
            dma((nz, n)), dma((nz, n)),
            dma((nz, n)), dma((nz, n)),
            dma((nz,)), dma((nz,)),
            dma((nz, n)), dma((nz, n)),
            dma((nz, n, n)), dma((nz, n, n)),
            dma((1,)), dma((1,)),
            dma((1,)), dma((1,)),
        ],
        compiler_params=pltpu.CompilerParams(
            collective_id=0, has_side_effects=True, vmem_limit_bytes=60 * 1024 * 1024
        ),
        cost_estimate=pl.CostEstimate(flops=10**9, bytes_accessed=10**7, transcendentals=10**5),
        name="decode",
    )(
        route_ids.T, route_weight.T, moe_input, queries[0], keys[0], values[0], w_up,
        jnp.swapaxes(w_down, 1, 2),
    )
    return (moe, ctx[None])


def solution(mesh):
    placed = (
        P(("req", "head"), "exp"),
        P(("req", "head"), None),
        P(("req", "head"), None),
        P("exp", ("req", "head"), None),
        P("exp", None, ("req", "head")),
        P(("req", "head", "exp"), None, None),
        P(("req", "head", "exp"), None, None),
        P(("req", "head", "exp"), None, None),
    )
    return jax.shard_map(
        shards,
        mesh=mesh,
        in_specs=placed,
        out_specs=(P(("req", "head"), "exp"), P(("req", "head", "exp"), None, None)),
        check_vma=False,
    )
```

time: 1100 us -> 90.1 us (0.08)
  waiting for transfers between devices: 652 us -> 0 us
  blocking collectives: 308 us -> 0 us
  Pallas kernels: 0 us -> 86.5 us
  starting transfers between devices: 57.4 us -> 0 us
  local copies, waits for them, and re-layouts: 52.7 us -> 2.73 us
  between operations: 14.2 us -> 0.64 us
    all_gather x2 -> x0, waiting for transfers between devices: 641 us -> none  [the longest x1 336 us: shards(): everyone = lax.all_gather(outgoing, ('req', 'head'), axis=2, tiled=True)]
    all_to_all x2 -> x0, blocking collectives: 308 us -> none  [the longest x1 291 us: shards(): lax.all_to_all(everyone, 'exp', split_axis=0, concat_axis=3, tiled=True)]
    pallas_call x0 -> x1, Pallas kernels: none -> 86.5 us  [shards(): pl.pallas_call(functools.partial(kernel, n, nz), out_shape=(jax.ShapeDtyp...]
    all_to_all x1 -> x0, starting transfers between devices: 57.3 us -> none  [shards(): lax.all_to_all(lax.all_to_all(result, ('req', 'head'), split_axis=1, conc...]
    all_to_all x3 -> x0, local copies, waits for them, and re-layouts: 19.9 us -> none  [the longest x1 8.44 us: shards(): lax.all_to_all(lax.all_to_all(result, ('req', 'head'), split_axis=1, conc...]
    unnamed x15 -> x2, local copies, waits for them, and re-layouts: 18.9 us -> 2.73 us
  transfers between devices with their start and end apart: 3 -> 0, of which waited for: 3 -> 0; matrix products, arithmetic and copies ran while one was open for 0% -> 0% of each run, Pallas kernels for 0% -> 0%
where the time goes in v2:
time: 90.1 us; the launch traced here: 89.9 us
  Pallas kernels  86.5 us (96%)
  local copies, waits for them, and re-layouts  2.73 us (3%)
    pallas_call x1, Pallas kernels, shards(): pl.pallas_call(functools.partial(kernel, n, nz), out_shape=(jax.ShapeDtyp...  86.5 us
    unnamed x2, local copies, waits for them, and re-layouts  2.73 us

profile of v2, /device:TPU:1, one launch (start us, length us, event | category | flops | bytes accessed | tf_op | source)
XLA Modules:
  0.0 89.9 jit_solution(2843623964095716877)
XLA Ops:
  0.6 86.5 %decode.1 = (bf16[12,896]{1,0:T(8,128)(2,1)}, bf16[64,256]{1,0:T(8,128)(2,1)}) custom-call(s32[3,12]{1,0:T(4,128)} %bitcast.12, f32[3,12]{1,0:T(4,128)} %bitcast.13, bf16[12,896]{1,0:T(8,128)(2,1)} %x_hbm.1, bf16[64,256]{1,0:T(8,128)(2,1)} %bitcast.10, bf16[1024,256]{1,0:T(8,128)(2,1)} %bitcast.8, bf16[1024,256]{1,0:T(8,128)(2,1)} %bitcast.9, ...), custom_call_target="tpu_custom_call" | custom-call | flops 1000000000 | bytes 10000000 | tf_op jit(solution)/shard_map/decode/pallas_call | solution.py:456
  87.1 1.4 %copy.12 = bf16[12,896]{1,0:T(8,128)(2,1)} copy(bf16[12,896]{1,0:T(8,128)(2,1)} %get-tuple-element.8) | data formatting | bytes 43008
  88.5 1.4 %copy.13 = bf16[1,64,256]{2,1,0:T(8,128)(2,1)} copy(bf16[1,64,256]{2,1,0:T(8,128)(2,1)} %bitcast.11) | data formatting | bytes 65536

commit v3 on v2

--- a/solution.py
+++ b/solution.py
@@ -37,11 +37,11 @@
     n, nz,
     ids_ref, wt_ref, x_hbm, q_hbm, k_hbm, v_hbm, up_hbm, down_hbm,
     out_ref, ctx_ref,
-    x_ref, q_ref, k_ref, v_ref, down_ref, up_ref, upcat_ref, wd_ref,
+    x_ref, q_ref, k_ref, v_ref, down_ref, up_ref, upcat_ref, wt_own, wd_ref,
     tok_ref, ids_pad, send1_ref, recv1_ref, xg_ref, part_ref, partin_ref,
-    hg_ref, acc_ref, r1s_ref, r1r_ref, r2r_ref,
+    hg_ref, acc_ref, r1s_ref, r1r_ref, r2s_ref, r2r_ref,
     loc_sem, up_s, up_r, s1_s, s1_r, s2_s, s2_r, s3_s, s3_r,
-    pt_s, pt_r, hz_s, hz_r, hg_s, hg_r, ho_s, ho_r,
+    pt_s, pt_r, wd_s, wd_r, hz_s, hz_r, ho_s, ho_r,
     r1_s, r1_r, r2_s, r2_r,
 ):
     toks, width = x_ref.shape
@@ -220,15 +220,29 @@
     batch = min(16, srcs)
 
     def spread_down(i):
-        for k in range(3):
-            t = down_ref[k, :, i * batch * fs:(i + 1) * batch * fs].astype(F32).T
-            for s in range(batch):
-                parts = [t[s * fs:(s + 1) * fs]]
-                if k:
-                    parts = [jnp.zeros((k * fs, dn), F32)] + parts
-                parts.append(jnp.zeros((128 - (k + 1) * fs, dn), F32))
-                at = (i * batch + s) * 128
-                wd_ref[at:at + 128, k * 128:k * 128 + dn] = jnp.concatenate(parts, axis=0).astype(BF)
+        t = [down_ref[k, :, i * batch * fs:(i + 1) * batch * fs].astype(F32).T for k in range(3)]
+        for s in range(batch):
+            parts = [t[k][s * fs:(s + 1) * fs] for k in range(3)]
+            parts.append(jnp.zeros((128 - 3 * fs, dn), F32))
+            at = i * batch + s
+            xs, ys = (at // nz) % n, at // nz // n
+            gs, os = xs * (1 - c) + ys * c, ys * (1 - c) + xs * c
+            row = pl.multiple_of((os * nz + at % nz) * 128, 128)
+            wt_own[gs, pl.ds(row, 128), 0:dn] = jnp.concatenate(parts, axis=0).astype(BF)
+
+    load_down.wait()
+    wt_own[...] = jnp.zeros_like(wt_own)
+    for i in range(srcs // batch):
+        spread_down(i)
+
+    def wd_part(g_):
+        return wd_ref.at[:, pl.ds(pl.multiple_of(g_ * 128, 128), 128)]
+
+    for d in hops:
+        p = add(g, d)
+        send(wt_own.at[p], wd_part(g), wd_s.at[d], wd_r.at[d], at_group(d))
+    keep_wd = pltpu.make_async_copy(wt_own.at[g], wd_part(g), loc_sem.at[8])
+    keep_wd.start()
 
     ru = lax.broadcasted_iota(I32, (chunks, unit, g2 * 48), 1)
     ch = lax.broadcasted_iota(I32, (chunks, unit, g2 * 48), 0)
@@ -251,11 +265,6 @@
         return lambda d: xg_ref.at[add(o, d), add(zl, nz - dz, nz)]
 
     spread(own, at_other, s3_s.at[0], s3_r.at[0])
-    load_down.wait()
-    wd_ref[...] = jnp.zeros_like(wd_ref)
-    batches = srcs // batch
-    for i in range((batches + 1) // 2):
-        spread_down(i)
     for dz in range(1, nz):
         block = x_from(dz)(0)
         arrived(block, s2_r.at[dz])
@@ -302,9 +311,9 @@
             )
         products(g, zs)
 
-    for i in range((batches + 1) // 2, batches):
-        spread_down(i)
-
+    rn = iota((rows, rows), 0)
+    src = ((rn // (2 * nz * n)) * nz + (rn % (2 * nz)) // 2) * g2 + ((rn // (2 * nz)) % n) * 2 + rn % 2
+    order = onehot(iota((rows, rows), 1) == src)
     raised = part_ref[g]
     for d in hops:
         for dz in range(nz):
@@ -313,68 +322,62 @@
     raised = raised.reshape(rows, 128)
     hidden = (raised / (1.0 + jnp.exp(-raised))).astype(BF)
 
-    def hpiece(g_, o_, z_):
-        return hg_ref.at[g_, o_, :, pl.ds(pl.multiple_of(z_ * 128, 128), 128)]
-
-    def g_from(dz):
-        return lambda d: hpiece(add(g, d), o, add(zl, nz - dz, nz))
-
-    def lower(g_, o_):
-        r_ = rid(g_, o_, c)
-        w = wd_ref[pl.ds(pl.multiple_of(r_ * (nz * 128), 128), nz * 128), :]
-        acc_ref[...] += dot(hg_ref[g_, o_], w)
-
-    hg_ref[g, o, :, pl.ds(pl.multiple_of(zl * 128, 128), 128)] = hidden
-    own = hpiece(g, o, zl)
+    hidden = dot(order, hidden).astype(BF)
+
+    def hpiece(o_, z_):
+        return hg_ref.at[o_, :, pl.ds(pl.multiple_of(z_ * 128, 128), 128)]
+
+    hg_ref[o, :, pl.ds(pl.multiple_of(zl * 128, 128), 128)] = hidden
+    own = hpiece(o, zl)
     for d in range(1, nz):
         send(own, own, hz_s.at[d], hz_r.at[d], dev(req, add(zl, d, nz), ex))
-    spread(own, at_group, hg_s.at[0], hg_r.at[0])
-    spread(own, at_other, ho_s.at[0, 0], ho_r.at[0, 0])
+    spread(own, at_other, ho_s.at[0], ho_r.at[0])
     acc_ref[...] = jnp.zeros_like(acc_ref)
     for dz in range(1, nz):
-        piece = g_from(dz)(0)
+        piece = hpiece(o, add(zl, nz - dz, nz))
         arrived(piece, hz_r.at[dz])
-        spread(piece, at_group, hg_s.at[dz], hg_r.at[dz])
-        spread(piece, at_other, ho_s.at[dz, 0], ho_r.at[dz, 0])
-    for dz in range(nz):
-        for dg in hops:
-            piece = g_from(dz)(n - dg)
-            arrived(piece, hg_r.at[dz, dg])
-            spread(piece, at_other, ho_s.at[dz, dg], ho_r.at[dz, dg])
-    for dg in range(n):
-        lower(add(g, n - dg), o)
-    for dg in (0,) + hops:
-        gs = add(g, n - dg)
-        for d in hops:
-            os = add(o, n - d)
-            for dz in range(nz):
-                arrived(hpiece(gs, os, add(zl, nz - dz, nz)), ho_r.at[dz, dg, d])
-            lower(gs, os)
-
-    ro = iota((plane * nz * 8, rows), 0)
-    co = iota((plane * nz * 8, rows), 1)
-    low = ro % 8
-    zt = (ro // 8) % nz
-    spot_of = ro // (8 * nz)
-    match = co - low % 2 == (((spot_of // n) * nz + zt) * n + spot_of % n) * 2
-    picked = jnp.zeros((plane * nz * 8, 128), F32)
+        spread(piece, at_other, ho_s.at[dz], ho_r.at[dz])
+
+    unit_of = iota((1, nz * 128), 1) % 128
+    masks = [onehot(jnp.logical_and(unit_of >= k * fs, unit_of < (k + 1) * fs)) for k in range(3)]
+
+    def lower(o_):
+        h = hg_ref[o_]
+        w = wd_ref[pl.ds(pl.multiple_of(o_ * (nz * 128), 128), nz * 128), :]
+        for k in range(3):
+            acc_ref[k] += dot(h * masks[k], w)
+
+    keep_wd.wait()
+    for d in hops:
+        arrived(wd_part(add(g, n - d)), wd_r.at[d])
+    lower(o)
+    for d in (1, 3, 2) if n == 4 else hops:
+        os = add(o, n - d)
+        for dz in range(nz):
+            arrived(hpiece(os, add(zl, nz - dz, nz)), ho_r.at[dz, d])
+        lower(os)
+
+    rz = 2 * nz
     for k in range(3):
-        take = onehot(jnp.logical_and(match, low // 2 == k))
-        picked = picked + dot(take, acc_ref[:, k * 128:(k + 1) * 128].astype(BF))
-    r1s_ref[...] = picked.reshape(plane, nz, 8, 128).astype(BF)
+        r1s_ref[:, k] = acc_ref[k].reshape(plane, rz, n * 128).astype(BF)
     spot = o * n + g
 
     def r1_send(d, carry):
         i = add(spot, d, plane)
         remote(
-            r1s_ref.at[i], r1r_ref.at[:, req], r1_s.at[0], r1_r.at[0],
+            r1s_ref.at[i], r1r_ref.at[req], r1_s.at[0], r1_r.at[0],
             dev(rid(i % n, i // n, c), zl, ex),
         ).start()
         return carry
 
     lax.fori_loop(1, plane, r1_send, 0)
-    keep = pltpu.make_async_copy(r1s_ref.at[spot], r1r_ref.at[:, req], loc_sem.at[6])
+    keep = pltpu.make_async_copy(r1s_ref.at[spot], r1r_ref.at[req], loc_sem.at[6])
     keep.start()
+
+    ro = iota((nz * 8, 32), 0)
+    low = ro % 8
+    order = onehot(jnp.logical_and(
+        iota((nz * 8, 32), 1) == (low // 2) * rz + (ro // 8) * 2 + low % 2, low < 6))
 
     rw = iota((g2 * mr, 128), 0)
     low = rw % 8
@@ -399,11 +402,23 @@
 
     keep.wait()
     arrived(r1s_ref.at[pl.ds(0, plane - 1)], r1_r.at[0])
+    for os in range(n):
+        whole = r1r_ref[rid(0, os, c)].astype(F32)
+        for gs in range(1, n):
+            whole = whole + r1r_ref[rid(gs, os, c)].astype(F32)
+        whole = whole.reshape(3 * rz, n * 128)
+        if rz < 8:
+            whole = jnp.concatenate([whole, jnp.zeros((32 - 3 * rz, n * 128), F32)], axis=0)
+        else:
+            whole = jnp.concatenate([whole, jnp.zeros((8, n * 128), F32)], axis=0)
+        whole = dot(order, whole.astype(BF))
+        for gd in range(n):
+            r2s_ref[:, rid(gd, os, c)] = whole[:, gd * 128:(gd + 1) * 128].reshape(nz, 8, 128).astype(BF)
     spot2 = zl * g2 + ex
 
     def r2_src(i):
         e2 = i % g2
-        return r1r_ref.at[i // g2, pl.ds((e2 // 2) * n + (e2 % 2) * hn, hn)]
+        return r2s_ref.at[i // g2, pl.ds((e2 // 2) * n + (e2 % 2) * hn, hn)]
 
     def r2_send(d, carry):
         i = add(spot2, d, column)
@@ -469,7 +484,8 @@
             pltpu.VMEM((3, dn, ffh), BF),
             pltpu.VMEM((n, 3, fs, dq), BF),
             pltpu.VMEM((n, 256, width), BF),
-            pltpu.VMEM((n * n * nz * 128, 384), BF),
+            pltpu.VMEM((n, n * nz * 128, 128), BF),
+            pltpu.VMEM((n * nz * 128, n * 128), BF),
             pltpu.VMEM((128, 128), BF),
             pltpu.VMEM((128, 128), F32),
             pltpu.VMEM((96 * n, 128), BF),
@@ -477,25 +493,26 @@
             pltpu.VMEM((n, nz, 12 * n, width), BF),
             pltpu.VMEM((n, n, nz, 2 * n, 128), F32),
             pltpu.VMEM((n - 1, n, nz, 2 * n, 128), F32),
-            pltpu.VMEM((n, n, rows, nz * 128), BF),
-            pltpu.VMEM((rows, 384), F32),
-            pltpu.VMEM((plane, nz, 8, 128), BF),
+            pltpu.VMEM((n, rows, nz * 128), BF),
+            pltpu.VMEM((3, rows, n * 128), F32),
+            pltpu.VMEM((plane, 3, 2 * nz, n * 128), BF),
+            pltpu.VMEM((plane, 3, 2 * nz, n * 128), BF),
             pltpu.VMEM((nz, plane, 8, 128), BF),
             pltpu.VMEM((2 * n * nz, n // 2, 8, 128), BF),
-            dma((8,)),
+            dma((9,)),
             dma((n,)), dma((n,)),
             dma((2 * n,)), dma((2 * n,)),
             dma((nz,)), dma((nz,)),
             dma((nz, n)), dma((nz, n)),
             dma((nz, n)), dma((nz, n)),
+            dma((n,)), dma((n,)),
             dma((nz,)), dma((nz,)),
             dma((nz, n)), dma((nz, n)),
-            dma((nz, n, n)), dma((nz, n, n)),
             dma((1,)), dma((1,)),
             dma((1,)), dma((1,)),
         ],
         compiler_params=pltpu.CompilerParams(
-            collective_id=0, has_side_effects=True, vmem_limit_bytes=60 * 1024 * 1024
+            collective_id=0, has_side_effects=True, vmem_limit_bytes=55 * 1024 * 1024
         ),
         cost_estimate=pl.CostEstimate(flops=10**9, bytes_accessed=10**7, transcendentals=10**5),
         name="decode",

time: 90.1 us -> 83.7 us (0.929)
  Pallas kernels: 86.5 us -> 80.1 us
    pallas_call x1, Pallas kernels: 86.5 us -> 80.1 us  [shards(): pl.pallas_call(functools.partial(kernel, n, nz), out_shape=(jax.ShapeDtyp...]
where the time goes in v3:
time: 83.7 us; the launch traced here: 83.4 us
  Pallas kernels  80.1 us (96%)
  local copies, waits for them, and re-layouts  2.73 us (3%)
    pallas_call x1, Pallas kernels, shards(): pl.pallas_call(functools.partial(kernel, n, nz), out_shape=(jax.ShapeDtyp...  80.1 us
    unnamed x2, local copies, waits for them, and re-layouts  2.73 us

profile of v3, /device:TPU:1, one launch (start us, length us, event | category | flops | bytes accessed | tf_op | source)
XLA Modules:
  0.0 83.4 jit_solution(5779989876668053579)
XLA Ops:
  0.6 80.1 %decode.1 = (bf16[12,896]{1,0:T(8,128)(2,1)}, bf16[64,256]{1,0:T(8,128)(2,1)}) custom-call(s32[3,12]{1,0:T(4,128)} %bitcast.12, f32[3,12]{1,0:T(4,128)} %bitcast.13, bf16[12,896]{1,0:T(8,128)(2,1)} %x_hbm.1, bf16[64,256]{1,0:T(8,128)(2,1)} %bitcast.10, bf16[1024,256]{1,0:T(8,128)(2,1)} %bitcast.8, bf16[1024,256]{1,0:T(8,128)(2,1)} %bitcast.9, ...), custom_call_target="tpu_custom_call" | custom-call | flops 1000000000 | bytes 10000000 | tf_op jit(solution)/shard_map/decode/pallas_call | solution.py:471
  80.7 1.4 %copy.12 = bf16[12,896]{1,0:T(8,128)(2,1)} copy(bf16[12,896]{1,0:T(8,128)(2,1)} %get-tuple-element.8) | data formatting | bytes 43008
  82.1 1.4 %copy.13 = bf16[1,64,256]{2,1,0:T(8,128)(2,1)} copy(bf16[1,64,256]{2,1,0:T(8,128)(2,1)} %bitcast.11) | data formatting | bytes 65536

commit v4 on v3

--- a/solution.py
+++ b/solution.py
@@ -69,6 +69,9 @@
     def dev(r_, zl_, ex_):
         return {"req": r_, "head": zl_, "exp": ex_}
 
+    def turned(z, f):
+        return z + f * (1 - 2 * (z % 2)) if nz > 1 else z
+
     def remote(src, dst, ss, rs, where):
         return pltpu.make_async_remote_copy(
             src_ref=src, dst_ref=dst, send_sem=ss, recv_sem=rs,
@@ -80,6 +83,9 @@
 
     def add(v, d, m=n):
         return (v + d) % m
+
+    away = (zh - g + n) % n
+    odd = (away // 2) * (1 - away % 2) if n == 4 else away
 
     sends = []
 
@@ -121,9 +127,6 @@
         greet(dev(req, m // g2, m % g2))
         return carry
 
-    lax.fori_loop(1, column, greet_column, 0)
-    lax.fori_loop(1, plane, greet_plane, 0)
-
     targets = []
     for dz in hops + (0,):
         for dt in range(2):
@@ -131,7 +134,7 @@
             g_t = x * (1 - t) + y * t
             o_t = y * (1 - t) + x * t
             zt = add(zh, dz)
-            targets.append((t, g_t, zt, dev(rid(zh, o_t, t), zl, zt * 2 + t), dt == 0 and dz == 0))
+            targets.append((t, g_t, zt, dev(rid(zh, o_t, t), turned(zl, 1 if dz == n // 2 else 0), zt * 2 + t), dt == 0 and dz == 0))
     home = g == zh
     for t, g_t, zt, where, own in targets:
         if own:
@@ -144,13 +147,16 @@
         cs = (c + dt) % 2
         for dg in range(n):
             gs = add(g, dg)
-            where = dev(rid(gs, o, c), zl, g * 2 + cs)
+            where = dev(rid(gs, o, c), turned(zl, odd), g * 2 + cs)
             if dt == 0 and dg == 0:
                 @pl.when(jnp.logical_not(home))
                 def _():
                     greet(where)
             else:
                 greet(where)
+
+    lax.fori_loop(1, column, greet_column, 0)
+    lax.fori_loop(1, plane, greet_plane, 0)
 
     ids_pad[...] = jnp.zeros_like(ids_pad)
     ids_pad[0:3, 0:toks] = (ids_ref[...] + 1).astype(F32)
@@ -238,9 +244,10 @@
     def wd_part(g_):
         return wd_ref.at[:, pl.ds(pl.multiple_of(g_ * 128, 128), 128)]
 
-    for d in hops:
-        p = add(g, d)
-        send(wt_own.at[p], wd_part(g), wd_s.at[d], wd_r.at[d], at_group(d))
+    def send_wd(d):
+        send(wt_own.at[add(g, d)], wd_part(g), wd_s.at[d], wd_r.at[d], at_group(d))
+
+    send_wd(hops[0])
     keep_wd = pltpu.make_async_copy(wt_own.at[g], wd_part(g), loc_sem.at[8])
     keep_wd.start()
 
@@ -255,14 +262,14 @@
         arrived(recv1_ref.at[pl.ds(i * 48, 48), :], s1_r.at[i])
     placed = dot(order, recv1_ref[...]).astype(BF)
     for ch in range(chunks):
-        xg_ref[o, zl, :, ch * 128:(ch + 1) * 128] = placed[ch * unit:(ch + 1) * unit]
-
-    own = xg_ref.at[o, zl]
+        xg_ref[o, turned(zl, odd), :, ch * 128:(ch + 1) * 128] = placed[ch * unit:(ch + 1) * unit]
+
+    own = xg_ref.at[o, turned(zl, odd)]
     for d in range(1, nz):
         send(own, own, s2_s.at[d], s2_r.at[d], dev(req, add(zl, d, nz), ex))
 
     def x_from(dz):
-        return lambda d: xg_ref.at[add(o, d), add(zl, nz - dz, nz)]
+        return lambda d: xg_ref.at[add(o, d), turned(add(zl, nz - dz, nz), odd)]
 
     spread(own, at_other, s3_s.at[0], s3_r.at[0])
     for dz in range(1, nz):
@@ -301,7 +308,7 @@
     for dz in range(nz):
         for d in hops:
             arrived(x_from(dz)(n - d), s3_r.at[dz, d])
-        zs = add(zl, nz - dz, nz)
+        zs = turned(add(zl, nz - dz, nz), odd)
         for d in hops:
             p = add(g, d)
             products(p, zs)
@@ -310,6 +317,9 @@
                 pt_s.at[dz, d], pt_r.at[dz, d], at_group(d),
             )
         products(g, zs)
+
+    for d in hops[1:]:
+        send_wd(d)
 
     rn = iota((rows, rows), 0)
     src = ((rn // (2 * nz * n)) * nz + (rn % (2 * nz)) // 2) * g2 + ((rn // (2 * nz)) % n) * 2 + rn % 2

time: 83.7 us -> 81.2 us (0.970)
  Pallas kernels: 80.1 us -> 77.6 us
    pallas_call x1, Pallas kernels: 80.1 us -> 77.6 us  [shards(): pl.pallas_call(functools.partial(kernel, n, nz), out_shape=(jax.ShapeDtyp...]
where the time goes in v4:
time: 81.2 us; the launch traced here: 80.9 us
  Pallas kernels  77.6 us (96%)
  local copies, waits for them, and re-layouts  2.73 us (3%)
    pallas_call x1, Pallas kernels, shards(): pl.pallas_call(functools.partial(kernel, n, nz), out_shape=(jax.ShapeDtyp...  77.6 us
    unnamed x2, local copies, waits for them, and re-layouts  2.73 us

profile of v4, /device:TPU:1, one launch (start us, length us, event | category | flops | bytes accessed | tf_op | source)
XLA Modules:
  0.0 80.9 jit_solution(2742260751743592628)
XLA Ops:
  0.6 77.6 %decode.1 = (bf16[12,896]{1,0:T(8,128)(2,1)}, bf16[64,256]{1,0:T(8,128)(2,1)}) custom-call(s32[3,12]{1,0:T(4,128)} %bitcast.12, f32[3,12]{1,0:T(4,128)} %bitcast.13, bf16[12,896]{1,0:T(8,128)(2,1)} %x_hbm.1, bf16[64,256]{1,0:T(8,128)(2,1)} %bitcast.10, bf16[1024,256]{1,0:T(8,128)(2,1)} %bitcast.8, bf16[1024,256]{1,0:T(8,128)(2,1)} %bitcast.9, ...), custom_call_target="tpu_custom_call" | custom-call | flops 1000000000 | bytes 10000000 | tf_op jit(solution)/shard_map/decode/pallas_call | solution.py:481
  78.2 1.4 %copy.12 = bf16[12,896]{1,0:T(8,128)(2,1)} copy(bf16[12,896]{1,0:T(8,128)(2,1)} %get-tuple-element.8) | data formatting | bytes 43008
  79.6 1.4 %copy.13 = bf16[1,64,256]{2,1,0:T(8,128)(2,1)} copy(bf16[1,64,256]{2,1,0:T(8,128)(2,1)} %bitcast.11) | data formatting | bytes 65536

commit v5 on v4

--- a/solution.py
+++ b/solution.py
@@ -375,7 +375,7 @@
     def r1_send(d, carry):
         i = add(spot, d, plane)
         remote(
-            r1s_ref.at[i], r1r_ref.at[req], r1_s.at[0], r1_r.at[0],
+            r1s_ref.at[i], r1r_ref.at[req], r1_s.at[0], r1_r.at[o],
             dev(rid(i % n, i // n, c), zl, ex),
         ).start()
         return carry
@@ -410,38 +410,43 @@
     p1 = (both - p0).astype(BF).astype(F32)
     parts = jnp.concatenate([p0, p1, both - p0 - p1], axis=0).astype(BF)
 
+    spot2 = zl * g2 + ex
     keep.wait()
-    arrived(r1s_ref.at[pl.ds(0, plane - 1)], r1_r.at[0])
-    for os in range(n):
-        whole = r1r_ref[rid(0, os, c)].astype(F32)
-        for gs in range(1, n):
-            whole = whole + r1r_ref[rid(gs, os, c)].astype(F32)
-        whole = whole.reshape(3 * rz, n * 128)
-        if rz < 8:
+    mate = o + 1 - 2 * (o % 2)
+    pairs = [(o, mate)] + ([(add(o, 2), add(mate, 2))] if n == 4 else [])
+    for at, pair in enumerate(pairs):
+        for here, os in enumerate(pair):
+            own = at == 0 and here == 0
+            arrived(r1s_ref.at[pl.ds(0, n - 1 if own else n)], r1_r.at[os])
+            whole = r1r_ref[rid(0, os, c)].astype(F32)
+            for gs in range(1, n):
+                whole = whole + r1r_ref[rid(gs, os, c)].astype(F32)
+            whole = whole.reshape(3 * rz, n * 128)
             whole = jnp.concatenate([whole, jnp.zeros((32 - 3 * rz, n * 128), F32)], axis=0)
-        else:
-            whole = jnp.concatenate([whole, jnp.zeros((8, n * 128), F32)], axis=0)
-        whole = dot(order, whole.astype(BF))
-        for gd in range(n):
-            r2s_ref[:, rid(gd, os, c)] = whole[:, gd * 128:(gd + 1) * 128].reshape(nz, 8, 128).astype(BF)
-    spot2 = zl * g2 + ex
-
-    def r2_src(i):
-        e2 = i % g2
-        return r2s_ref.at[i // g2, pl.ds((e2 // 2) * n + (e2 % 2) * hn, hn)]
-
-    def r2_send(d, carry):
-        i = add(spot2, d, column)
-        remote(
-            r2_src(i), r2r_ref.at[spot2], r2_s.at[0], r2_r.at[0], dev(req, i // g2, i % g2)
-        ).start()
-        return carry
-
-    lax.fori_loop(1, column, r2_send, 0)
-    keep = pltpu.make_async_copy(r2_src(spot2), r2r_ref.at[spot2], loc_sem.at[7])
-    keep.start()
-    keep.wait()
-    arrived(r2r_ref.at[pl.ds(0, column - 1)], r2_r.at[0])
+            whole = dot(order, whole.astype(BF))
+            for gd in range(n):
+                r2s_ref[:, rid(gd, os, c)] = whole[:, gd * 128:(gd + 1) * 128].reshape(nz, 8, 128).astype(BF)
+
+        def r2_send(i, carry):
+            zt, rest = i // n, i % n
+            y2 = (pair[0] // 2 * 2 + rest // hn) * (1 - c) + rest * c
+            x2 = (rest % hn) * (1 - c) + (pair[0] // 2) * c
+            e2 = y2 * 2 + x2
+            src = r2s_ref.at[zt, pl.ds(y2 * n + x2 * hn, hn)]
+            mine = zt * g2 + e2 == spot2
+
+            @pl.when(mine)
+            def _():
+                pltpu.make_async_copy(src, r2r_ref.at[spot2], r2_r.at[0]).start()
+
+            @pl.when(jnp.logical_not(mine))
+            def _():
+                remote(src, r2r_ref.at[spot2], r2_s.at[0], r2_r.at[0], dev(req, zt, e2)).start()
+
+            return carry
+
+        lax.fori_loop(0, n * nz, r2_send, 0)
+    arrived(r2r_ref, r2_r.at[0])
 
     sums = [dot(parts, r2r_ref[z * g2:(z + 1) * g2].astype(F32).reshape(g2 * mr, 128).astype(BF)) for z in range(nz)]
     sums = jnp.concatenate(sums, axis=1)
@@ -518,7 +523,7 @@
             dma((n,)), dma((n,)),
             dma((nz,)), dma((nz,)),
             dma((nz, n)), dma((nz, n)),
-            dma((1,)), dma((1,)),
+            dma((1,)), dma((n,)),
             dma((1,)), dma((1,)),
         ],
         compiler_params=pltpu.CompilerParams(

time: 81.2 us -> 80.1 us (0.986)
  Pallas kernels: 77.6 us -> 76.5 us
    pallas_call x1, Pallas kernels: 77.6 us -> 76.5 us  [shards(): pl.pallas_call(functools.partial(kernel, n, nz), out_shape=(jax.ShapeDtyp...]
where the time goes in v5:
time: 80.1 us; the launch traced here: 79.9 us
  Pallas kernels  76.5 us (96%)
  local copies, waits for them, and re-layouts  2.73 us (3%)
    pallas_call x1, Pallas kernels, shards(): pl.pallas_call(functools.partial(kernel, n, nz), out_shape=(jax.ShapeDtyp...  76.5 us
    unnamed x2, local copies, waits for them, and re-layouts  2.73 us

profile of v5, /device:TPU:1, one launch (start us, length us, event | category | flops | bytes accessed | tf_op | source)
XLA Modules:
  0.0 79.9 jit_solution(9828419718771070949)
XLA Ops:
  0.6 76.5 %decode.1 = (bf16[12,896]{1,0:T(8,128)(2,1)}, bf16[64,256]{1,0:T(8,128)(2,1)}) custom-call(s32[3,12]{1,0:T(4,128)} %bitcast.12, f32[3,12]{1,0:T(4,128)} %bitcast.13, bf16[12,896]{1,0:T(8,128)(2,1)} %x_hbm.1, bf16[64,256]{1,0:T(8,128)(2,1)} %bitcast.10, bf16[1024,256]{1,0:T(8,128)(2,1)} %bitcast.8, bf16[1024,256]{1,0:T(8,128)(2,1)} %bitcast.9, ...), custom_call_target="tpu_custom_call" | custom-call | flops 1000000000 | bytes 10000000 | tf_op jit(solution)/shard_map/decode/pallas_call | solution.py:486
  77.1 1.4 %copy.12 = bf16[12,896]{1,0:T(8,128)(2,1)} copy(bf16[12,896]{1,0:T(8,128)(2,1)} %get-tuple-element.8) | data formatting | bytes 43008
  78.5 1.4 %copy.13 = bf16[1,64,256]{2,1,0:T(8,128)(2,1)} copy(bf16[1,64,256]{2,1,0:T(8,128)(2,1)} %bitcast.11) | data formatting | bytes 65536

commit v6 on v5

--- a/solution.py
+++ b/solution.py
@@ -372,15 +372,15 @@
         r1s_ref[:, k] = acc_ref[k].reshape(plane, rz, n * 128).astype(BF)
     spot = o * n + g
 
-    def r1_send(d, carry):
-        i = add(spot, d, plane)
-        remote(
-            r1s_ref.at[i], r1r_ref.at[req], r1_s.at[0], r1_r.at[o],
-            dev(rid(i % n, i // n, c), zl, ex),
-        ).start()
-        return carry
-
-    lax.fori_loop(1, plane, r1_send, 0)
+    mate = o + 1 - 2 * (o % 2)
+    pairs = [(o, mate)] + ([(add(o, 2), add(mate, 2))] if n == 4 else [])
+    for at, os in enumerate(os for pair in pairs for os in pair):
+        for dg in range(0 if at else 1, n):
+            gs = add(g, dg)
+            remote(
+                r1s_ref.at[os * n + gs], r1r_ref.at[req], r1_s.at[0], r1_r.at[o],
+                dev(rid(gs, os, c), zl, ex),
+            ).start()
     keep = pltpu.make_async_copy(r1s_ref.at[spot], r1r_ref.at[req], loc_sem.at[6])
     keep.start()
 
@@ -412,8 +412,6 @@
 
     spot2 = zl * g2 + ex
     keep.wait()
-    mate = o + 1 - 2 * (o % 2)
-    pairs = [(o, mate)] + ([(add(o, 2), add(mate, 2))] if n == 4 else [])
     for at, pair in enumerate(pairs):
         for here, os in enumerate(pair):
             own = at == 0 and here == 0
@@ -446,6 +444,15 @@
             return carry
 
         lax.fori_loop(0, n * nz, r2_send, 0)
+    for cp in sends:
+        cp.wait_send()
+
+    @pl.when(jnp.logical_not(home))
+    def _():
+        first.wait_send()
+    arrived(r1s_ref.at[pl.ds(0, plane - 1)], r1_s.at[0])
+    arrived(r2r_ref.at[pl.ds(0, column - 1)], r2_s.at[0])
+
     arrived(r2r_ref, r2_r.at[0])
 
     sums = [dot(parts, r2r_ref[z * g2:(z + 1) * g2].astype(F32).reshape(g2 * mr, 128).astype(BF)) for z in range(nz)]
@@ -457,15 +464,6 @@
             pieces.append(sums[i * 16:i * 16 + toks, z * 128:z * 128 + dn])
     total = jnp.concatenate(pieces, axis=1)
     out_ref[...] = (x_ref[...].astype(F32) + total).astype(BF)
-
-    for cp in sends:
-        cp.wait_send()
-
-    @pl.when(jnp.logical_not(home))
-    def _():
-        first.wait_send()
-    arrived(r1s_ref.at[pl.ds(0, plane - 1)], r1_s.at[0])
-    arrived(r2r_ref.at[pl.ds(0, column - 1)], r2_s.at[0])
 
 
 def shards(moe_input, route_ids, route_weight, w_up, w_down, queries, keys, values):

time: 80.1 us -> 79.2 us (0.989)
  Pallas kernels: 76.5 us -> 75.5 us
    pallas_call x1, Pallas kernels: 76.5 us -> 75.5 us  [shards(): pl.pallas_call(functools.partial(kernel, n, nz), out_shape=(jax.ShapeDtyp...]
where the time goes in v6:
time: 79.2 us; the launch traced here: 78.9 us
  Pallas kernels  75.5 us (95%)
  local copies, waits for them, and re-layouts  2.73 us (3%)
    pallas_call x1, Pallas kernels, shards(): pl.pallas_call(functools.partial(kernel, n, nz), out_shape=(jax.ShapeDtyp...  75.5 us
    unnamed x2, local copies, waits for them, and re-layouts  2.73 us

profile of v6, /device:TPU:1, one launch (start us, length us, event | category | flops | bytes accessed | tf_op | source)
XLA Modules:
  0.0 78.9 jit_solution(4002722090870226286)
XLA Ops:
  0.6 75.5 %decode.1 = (bf16[12,896]{1,0:T(8,128)(2,1)}, bf16[64,256]{1,0:T(8,128)(2,1)}) custom-call(s32[3,12]{1,0:T(4,128)} %bitcast.12, f32[3,12]{1,0:T(4,128)} %bitcast.13, bf16[12,896]{1,0:T(8,128)(2,1)} %x_hbm.1, bf16[64,256]{1,0:T(8,128)(2,1)} %bitcast.10, bf16[1024,256]{1,0:T(8,128)(2,1)} %bitcast.8, bf16[1024,256]{1,0:T(8,128)(2,1)} %bitcast.9, ...), custom_call_target="tpu_custom_call" | custom-call | flops 1000000000 | bytes 10000000 | tf_op jit(solution)/shard_map/decode/pallas_call | solution.py:484
  76.2 1.4 %copy.12 = bf16[12,896]{1,0:T(8,128)(2,1)} copy(bf16[12,896]{1,0:T(8,128)(2,1)} %get-tuple-element.8) | data formatting | bytes 43008
  77.5 1.4 %copy.13 = bf16[1,64,256]{2,1,0:T(8,128)(2,1)} copy(bf16[1,64,256]{2,1,0:T(8,128)(2,1)} %bitcast.11) | data formatting | bytes 65536
